TPU v7x, 128 devices: a whole 4x4x4 slice. The times are simulated.
128 devices in a mesh: seq: 32 (over z, y_hi, x), tensor: 4 (over y_lo, core).
Axes of the slice: x: 4, y: 4 (y_hi: 2, y_lo: 2; y = y_hi * 2 + y_lo), z: 4, core: 2. Of those that a mesh axis runs over, the one named last changes fastest.
Arguments:
- inputs: bfloat16 [8192, 768], P('seq'), may hold values from -6 to 6
- head_weights: bfloat16 [3, 768, 768], P(None, None, 'tensor'), may hold values from -0.3125 to 0.3125
- out_weight: bfloat16 [768, 768], P('tensor'), may hold values from -0.21875 to 0.21875
- up_weight: bfloat16 [768, 3072], P(None, 'tensor'), may hold values from -0.21875 to 0.21875
- down_weight: bfloat16 [3072, 768], P('tensor'), may hold values from -0.109375 to 0.109375
- in_gain: float32 [768], replicated, may hold values from 0.1 to 1.9
- in_shift: float32 [768], replicated, may hold values from -1.5 to 1.5
- mix_gain: float32 [768], P('tensor'), may hold values from 0.1 to 1.9
- mix_shift: float32 [768], P('tensor'), may hold values from -1.5 to 1.5
- mid_gain: float32 [768], replicated, may hold values from 0.1 to 1.9
- mid_shift: float32 [768], replicated, may hold values from -1.5 to 1.5
- inner_gain: float32 [3072], P('tensor'), may hold values from 0.1 to 1.9
- inner_shift: float32 [3072], P('tensor'), may hold values from -1.5 to 1.5
- valid_length: int32 [1], replicated, may hold values from 8064 to 8192
- cotangent: bfloat16 [8192, 768], P('seq'), may hold values from -6 to 6
Outputs:
- result: bfloat16 [8192, 768], P('seq')
- inputs_grad: bfloat16 [8192, 768], P('seq')
- head_weights_grad: float32 [3, 768, 768], P(None, None, 'tensor')
- out_weight_grad: float32 [768, 768], P('tensor')
- up_weight_grad: float32 [768, 3072], P(None, 'tensor')
- down_weight_grad: float32 [3072, 768], P('tensor')
- in_gain_grad: float32 [768], replicated
- in_shift_grad: float32 [768], replicated
- mix_gain_grad: float32 [768], P('tensor')
- mix_shift_grad: float32 [768], P('tensor')
- mid_gain_grad: float32 [768], replicated
- mid_shift_grad: float32 [768], replicated
- inner_gain_grad: float32 [3072], P('tensor')
- inner_shift_grad: float32 [3072], P('tensor')
Inputs may be any that keep to these rules, and one draw needn't show every extreme that they name: Tokens at positions valid_length and above are padding.
All inputs are finite; a program needn't handle non-finite values.
Results may differ from a plain program's by a relative error of at most 0.03.
Values may be sent and summed in bfloat16 or wider, within the bound.
No kernel may reach another device: no remote copies, remote signals or barrier semaphores. Data moves between devices by JAX's collectives and lax.ppermute only.
A program may use at most 192 MiB of HBM per device.

v0:
```python
import jax
import jax.numpy as jnp
from jax import lax
from jax.sharding import PartitionSpec as P

HDIM = 64
SEG_A = 2048
SEG_B = 4096
SEG_C = 8192
SEG_D = 16384
SEG_E = 32768


EPSILON = 1e-05
DILATIONS = (1, 2, 4, 6, 12)


def pattern_weights(row_pos, col_pos, head_index, valid_count):
    segment_sizes = (SEG_A, SEG_B, SEG_C, SEG_D, SEG_E)
    weight_sum = jnp.zeros((row_pos.shape[0], col_pos.shape[0]), jnp.float32)
    for segment, dilation in zip(segment_sizes, DILATIONS):
        offset = head_index % dilation
        matches = row_pos[:, None] // segment == col_pos[None, :] // segment
        matches = (
            matches
            & (row_pos[:, None] % dilation == offset)
            & (col_pos[None, :] % dilation == offset)
        )
        weight_sum = weight_sum + matches.astype(jnp.float32)
    allowed = (col_pos[None, :] <= row_pos[:, None]) & (col_pos[None, :] < valid_count)
    return jnp.where(allowed, weight_sum, 0.0)


def norm_finish(values, first_sum, second_sum, count_width, norm_gain, norm_shift):
    row_mean = first_sum[:, None] / count_width
    spread = second_sum[:, None] / count_width - row_mean * row_mean
    scale_row = lax.rsqrt(spread + EPSILON)
    unit_rows = (values - row_mean) * scale_row
    return (unit_rows * norm_gain + norm_shift, unit_rows, scale_row)


def norm_back(upstream_grad, unit_rows, scale_row, norm_gain, first_sum, second_sum, count_width):
    return scale_row * (
        upstream_grad * norm_gain
        - first_sum[:, None] / count_width
        - unit_rows * second_sum[:, None] / count_width
    )


def local_norm(values, norm_gain, norm_shift):
    return norm_finish(
        values,
        jnp.sum(values, 1),
        jnp.sum(values * values, 1),
        values.shape[1],
        norm_gain,
        norm_shift,
    )


def local_norm_back(upstream_grad, unit_rows, scale_row, norm_gain):
    scaled = upstream_grad * norm_gain
    return norm_back(
        upstream_grad,
        unit_rows,
        scale_row,
        norm_gain,
        jnp.sum(scaled, 1),
        jnp.sum(scaled * unit_rows, 1),
        unit_rows.shape[1],
    )


def smooth(values):
    return jax.nn.gelu(values, approximate=True)


def score_block(queries, key_block):
    return jnp.einsum(
        "qe,ke->qk", queries, key_block, preferred_element_type=jnp.float32
    ) * HDIM ** (-0.5)


def per_device(
    inputs,
    head_weights,
    out_weight,
    up_weight,
    down_weight,
    in_gain,
    in_shift,
    mix_gain,
    mix_shift,
    mid_gain,
    mid_shift,
    inner_gain,
    inner_shift,
    valid_length,
    cotangent,
):
    tok_rows = inputs.shape[0]
    inner_width = up_weight.shape[1] * lax.axis_size("tensor")
    mix_width = out_weight.shape[0] * lax.axis_size("tensor")
    heads_here = out_weight.shape[0] // HDIM
    first_head = lax.axis_index("tensor") * heads_here
    valid_count = valid_length[0]
    positions = lax.axis_index("seq") * tok_rows + jnp.arange(tok_rows, dtype=jnp.int32)
    row_valid = (positions < valid_count)[:, None]
    source = inputs.astype(jnp.float32)
    normed, in_unit, in_scale = local_norm(source, in_gain, in_shift)
    normed_low = normed.astype(jnp.bfloat16)
    projected = jnp.einsum(
        "td,cde->cte", normed_low, head_weights, preferred_element_type=jnp.float32
    ).astype(jnp.bfloat16)
    gathered_pairs = lax.all_gather(projected[1:], "seq", axis=1, tiled=True)
    columns = jnp.arange(gathered_pairs.shape[1], dtype=jnp.int32)
    head_outputs = []
    log_totals = []
    for within in range(heads_here):
        head_start = within * HDIM
        queries = projected[0, :, head_start : head_start + HDIM]
        key_block = gathered_pairs[0, :, head_start : head_start + HDIM]
        value_block = gathered_pairs[1, :, head_start : head_start + HDIM]
        multiple = pattern_weights(positions, columns, first_head + within, valid_count)
        present = multiple > 0
        scores = score_block(queries, key_block)
        highest = jnp.max(jnp.where(present, scores, -1e30), axis=1, keepdims=True)
        weighted = multiple * jnp.exp(jnp.where(present, scores - highest, -10000.0))
        totals = jnp.sum(weighted, 1, keepdims=True)
        shares = (weighted / totals).astype(jnp.bfloat16)
        head_outputs.append(jnp.dot(shares, value_block, preferred_element_type=jnp.float32))
        log_totals.append(highest + jnp.log(totals))
    attended = jnp.concatenate(head_outputs, 1)
    mix_sums = lax.psum((jnp.sum(attended, 1), jnp.sum(attended * attended, 1)), "tensor")
    mix_normed, mix_unit, mix_scale = norm_finish(
        attended, mix_sums[0], mix_sums[1], mix_width, mix_gain, mix_shift
    )
    mix_low = mix_normed.astype(jnp.bfloat16)
    branch = lax.psum(
        jnp.dot(mix_low, out_weight, preferred_element_type=jnp.float32).astype(jnp.bfloat16),
        "tensor",
    ).astype(jnp.float32)
    hidden = source + branch
    mid_normed, mid_unit, mid_scale = local_norm(hidden, mid_gain, mid_shift)
    mid_low = mid_normed.astype(jnp.bfloat16)
    pre_act = jnp.dot(mid_low, up_weight, preferred_element_type=jnp.float32)
    active = smooth(pre_act)
    inner_sums = lax.psum((jnp.sum(active, 1), jnp.sum(active * active, 1)), "tensor")
    inner_normed, inner_unit, inner_scale = norm_finish(
        active, inner_sums[0], inner_sums[1], inner_width, inner_gain, inner_shift
    )
    inner_low = inner_normed.astype(jnp.bfloat16)
    feed_out = lax.psum(
        jnp.dot(inner_low, down_weight, preferred_element_type=jnp.float32).astype(jnp.bfloat16),
        "tensor",
    ).astype(jnp.float32)
    result = jnp.where(row_valid, hidden + feed_out, 0.0).astype(jnp.bfloat16)
    upstream = jnp.where(row_valid, cotangent.astype(jnp.float32), 0.0)
    feed_grad = upstream.astype(jnp.bfloat16)
    down_grad = jnp.einsum("tf,td->fd", inner_low, feed_grad, preferred_element_type=jnp.float32)
    inner_grad = jnp.einsum("td,fd->tf", feed_grad, down_weight, preferred_element_type=jnp.float32)
    inner_gain_grad = jnp.sum(inner_grad * inner_unit, 0)
    inner_shift_grad = jnp.sum(inner_grad, 0)
    inner_scaled = inner_grad * inner_gain
    inner_back = lax.psum(
        (jnp.sum(inner_scaled, 1), jnp.sum(inner_scaled * inner_unit, 1)), "tensor"
    )
    active_grad = norm_back(
        inner_grad, inner_unit, inner_scale, inner_gain, inner_back[0], inner_back[1], inner_width
    )
    pre_grad = jax.vjp(smooth, pre_act)[1](active_grad)[0].astype(jnp.bfloat16)
    up_grad = jnp.einsum("td,tf->df", mid_low, pre_grad, preferred_element_type=jnp.float32)
    mid_grad = lax.psum(
        jnp.einsum("tf,df->td", pre_grad, up_weight, preferred_element_type=jnp.float32).astype(
            jnp.bfloat16
        ),
        "tensor",
    ).astype(jnp.float32)
    mid_gain_grad = jnp.sum(mid_grad * mid_unit, 0)
    mid_shift_grad = jnp.sum(mid_grad, 0)
    hidden_grad = upstream + local_norm_back(mid_grad, mid_unit, mid_scale, mid_gain)
    branch_grad = hidden_grad.astype(jnp.bfloat16)
    out_grad = jnp.einsum("te,td->ed", mix_low, branch_grad, preferred_element_type=jnp.float32)
    mix_grad = jnp.einsum("td,ed->te", branch_grad, out_weight, preferred_element_type=jnp.float32)
    mix_gain_grad = jnp.sum(mix_grad * mix_unit, 0)
    mix_shift_grad = jnp.sum(mix_grad, 0)
    mix_scaled = mix_grad * mix_gain
    mix_back = lax.psum((jnp.sum(mix_scaled, 1), jnp.sum(mix_scaled * mix_unit, 1)), "tensor")
    attended_grad = norm_back(
        mix_grad, mix_unit, mix_scale, mix_gain, mix_back[0], mix_back[1], mix_width
    ).astype(jnp.bfloat16)
    backward_pairs = lax.all_gather(projected[1:], "seq", axis=1, tiled=True)
    query_parts = []
    key_parts = []
    value_parts = []
    for within in range(heads_here):
        head_start = within * HDIM
        queries = projected[0, :, head_start : head_start + HDIM]
        key_block = backward_pairs[0, :, head_start : head_start + HDIM]
        value_block = backward_pairs[1, :, head_start : head_start + HDIM]
        multiple = pattern_weights(positions, columns, first_head + within, valid_count)
        present = multiple > 0
        scores = score_block(queries, key_block)
        shares_full = multiple * jnp.exp(jnp.where(present, scores - log_totals[within], -10000.0))
        shares_low = shares_full.astype(jnp.bfloat16)
        head_grad_rows = attended_grad[:, head_start : head_start + HDIM]
        share_grad = jnp.einsum(
            "qe,ke->qk", head_grad_rows, value_block, preferred_element_type=jnp.float32
        )
        centre = jnp.sum(shares_full * share_grad, 1, keepdims=True)
        score_grad = (shares_full * (share_grad - centre)).astype(jnp.bfloat16)
        query_parts.append(
            jnp.dot(score_grad, key_block, preferred_element_type=jnp.float32) * HDIM ** (-0.5)
        )
        key_parts.append(
            jnp.einsum("qk,qe->ke", score_grad, queries, preferred_element_type=jnp.float32)
            * HDIM ** (-0.5)
        )
        value_parts.append(
            jnp.einsum("qk,qe->ke", shares_low, head_grad_rows, preferred_element_type=jnp.float32)
        )
    pair_terms = jnp.stack((jnp.concatenate(key_parts, 1), jnp.concatenate(value_parts, 1)))
    pair_grad = lax.psum_scatter(
        pair_terms.astype(jnp.bfloat16), "seq", scatter_dimension=1, tiled=True
    )
    query_grad = jnp.concatenate(query_parts, 1).astype(jnp.bfloat16)
    projected_grad = jnp.concatenate((query_grad[None], pair_grad), 0)
    head_grad = jnp.einsum(
        "td,cte->cde", normed_low, projected_grad, preferred_element_type=jnp.float32
    )
    normed_grad = lax.psum(
        jnp.einsum(
            "cte,cde->td", projected_grad, head_weights, preferred_element_type=jnp.float32
        ).astype(jnp.bfloat16),
        "tensor",
    ).astype(jnp.float32)
    in_gain_grad = jnp.sum(normed_grad * in_unit, 0)
    in_shift_grad = jnp.sum(normed_grad, 0)
    inputs_grad = (hidden_grad + local_norm_back(normed_grad, in_unit, in_scale, in_gain)).astype(
        jnp.bfloat16
    )
    summed = (
        lax.psum(head_grad.astype(jnp.bfloat16), "seq").astype(jnp.float32),
        lax.psum(out_grad.astype(jnp.bfloat16), "seq").astype(jnp.float32),
        lax.psum(up_grad.astype(jnp.bfloat16), "seq").astype(jnp.float32),
        lax.psum(down_grad.astype(jnp.bfloat16), "seq").astype(jnp.float32),
        lax.psum(in_gain_grad.astype(jnp.bfloat16), "seq").astype(jnp.float32),
        lax.psum(in_shift_grad.astype(jnp.bfloat16), "seq").astype(jnp.float32),
        lax.psum(mix_gain_grad.astype(jnp.bfloat16), "seq").astype(jnp.float32),
        lax.psum(mix_shift_grad.astype(jnp.bfloat16), "seq").astype(jnp.float32),
        lax.psum(mid_gain_grad.astype(jnp.bfloat16), "seq").astype(jnp.float32),
        lax.psum(mid_shift_grad.astype(jnp.bfloat16), "seq").astype(jnp.float32),
        lax.psum(inner_gain_grad.astype(jnp.bfloat16), "seq").astype(jnp.float32),
        lax.psum(inner_shift_grad.astype(jnp.bfloat16), "seq").astype(jnp.float32),
    )
    return (
        result,
        inputs_grad,
        summed[0],
        summed[1],
        summed[2],
        summed[3],
        summed[4],
        summed[5],
        summed[6],
        summed[7],
        summed[8],
        summed[9],
        summed[10],
        summed[11],
    )


def solution(mesh):
    in_specs = (
        P("seq", None),
        P(None, None, "tensor"),
        P("tensor", None),
        P(None, "tensor"),
        P("tensor", None),
        P(),
        P(),
        P("tensor"),
        P("tensor"),
        P(),
        P(),
        P("tensor"),
        P("tensor"),
        P(),
        P("seq", None),
    )
    out_specs = (
        P("seq", None),
        P("seq", None),
        P(None, None, "tensor"),
        P("tensor", None),
        P(None, "tensor"),
        P("tensor", None),
        P(),
        P(),
        P("tensor"),
        P("tensor"),
        P(),
        P(),
        P("tensor"),
        P("tensor"),
    )
    return jax.shard_map(
        per_device, mesh=mesh, in_specs=in_specs, out_specs=out_specs, check_vma=False
    )
```

profile of v0, /device:TPU:0, one launch (start us, length us, event | category | flops | bytes accessed | tf_op | source)
XLA Modules:
  0.0 1096.2 jit_solution(9378547913729564886)
XLA Ops:
  13.5 93.8 %all-gather.2.cloned.1.call-done = bf16[2,8192,192]{1,2,0:T(8,128)(2,1)} async-done(((bf16[2,256,192]{1,2,0:T(8,128)(2,1)}), bf16[2,8192,192]{1,2,0:T(8,128)(2,1)}) %all-gather.2.cloned.1.call-update) | async-done | bytes 6291472 | tf_op jit(solution)/shard_map/all_gather | solution.py:115
  107.3 11.7 %select_reduce_fusion = (f32[256]{0:T(256)S(1)}, f32[256,8192]{1,0:T(8,128)S(1)}) fusion(pred[8192]{0:T(1024)(128)(4,1)S(1)} %get-tuple-element.112, pred[256]{0:T(512)(128)(4,1)S(1)} %get-tuple-element.96, s32[8192]{0:T(1024)S(1)} %get-tuple-element.108, s32[256]{0:T(256)S(1)} %get-tuple-element.90, pred[8192]{0:T(1024)(128)(4,1)S(1)} %get-tuple-element.113, ...), kind=kOutput, calls=%fused_computation.50 | convolution fusion | flops 329252608 | bytes 9683968 | tf_op jit(solution)/shard_map/qe,ke->qk/dot_general | solution.py:79
  119.0 14.9 %fusion.138 = f32[256]{0:T(256)S(1)} fusion(f32[256,8192]{1,0:T(8,128)S(1)} %get-tuple-element.73, f32[256]{0:T(256)S(1)} %get-tuple-element.72, pred[8192]{0:T(1024)(128)(4,1)S(1)} %get-tuple-element.112, pred[256]{0:T(512)(128)(4,1)S(1)} %get-tuple-element.96, s32[8192]{0:T(1024)S(1)} %get-tuple-element.108, s32[256]{0:T(256)S(1)} %get-tuple-element.90, ...), kind=kLoop, calls=%fused_computation.312 | loop fusion | flops 62914304 | bytes 8602624 | tf_op jit(solution)/shard_map/reduce_sum | solution.py:129
  133.9 10.3 select_reduce_fusion.1
  144.2 13.9 %fusion.137 = f32[256]{0:T(256)S(1)} fusion(f32[256,8192]{1,0:T(8,128)S(1)} %get-tuple-element.75, f32[256]{0:T(256)S(1)} %get-tuple-element.74, pred[8192]{0:T(1024)(128)(4,1)S(1)} %get-tuple-element.116, pred[256]{0:T(512)(128)(4,1)S(1)} %get-tuple-element.100, s32[8192]{0:T(1024)S(1)} %get-tuple-element.108, s32[256]{0:T(256)S(1)} %get-tuple-element.90, ...), kind=kLoop, calls=%fused_computation.311 | loop fusion | flops 62914304 | bytes 8602624 | tf_op jit(solution)/shard_map/reduce_sum | solution.py:129
  158.1 10.3 select_reduce_fusion.2
  168.4 14.0 %fusion.136 = f32[256]{0:T(256)S(1)} fusion(f32[256,8192]{1,0:T(8,128)S(1)} %get-tuple-element.77, f32[256]{0:T(256)S(1)} %get-tuple-element.76, pred[8192]{0:T(1024)(128)(4,1)S(1)} %get-tuple-element.120, pred[256]{0:T(512)(128)(4,1)S(1)} %get-tuple-element.104, s32[8192]{0:T(1024)S(1)} %get-tuple-element.108, s32[256]{0:T(256)S(1)} %get-tuple-element.90, ...), kind=kLoop, calls=%fused_computation.310 | loop fusion | flops 62914304 | bytes 8602624 | tf_op jit(solution)/shard_map/reduce_sum | solution.py:129
  182.5 11.7 %fusion.143 = (f32[256]{0:T(256)S(1)}, f32[256,64]{0,1:T(8,128)S(1)}) fusion(bf16[2,8192,192]{1,2,0:T(8,128)(2,1)S(1)} %bitcast.105, f32[256]{0:T(256)S(1)} %fusion.138, f32[256,8192]{1,0:T(8,128)S(1)} %get-tuple-element.73, f32[256]{0:T(256)S(1)} %get-tuple-element.72, pred[8192]{0:T(1024)(128)(4,1)S(1)} %get-tuple-element.112, ...), kind=kOutput, calls=%fused_computation.314 | convolution fusion | flops 333463296 | bytes 9718272 | tf_op jit(solution)/shard_map/dot_general | solution.py:131
  194.3 11.2 %fusion.145 = (f32[256]{0:T(256)S(1)}, f32[256,64]{0,1:T(8,128)S(1)}) fusion(bf16[2,8192,192]{1,2,0:T(8,128)(2,1)S(1)} %bitcast.105, f32[256]{0:T(256)S(1)} %fusion.137, f32[256,8192]{1,0:T(8,128)S(1)} %get-tuple-element.75, f32[256]{0:T(256)S(1)} %get-tuple-element.74, pred[8192]{0:T(1024)(128)(4,1)S(1)} %get-tuple-element.116, ...), kind=kOutput, calls=%fused_computation.316 | convolution fusion | flops 333463296 | bytes 9718784 | tf_op jit(solution)/shard_map/dot_general | solution.py:131
  205.8 11.5 %fusion.144 = (f32[256]{0:T(256)S(1)}, f32[256,64]{0,1:T(8,128)S(1)}) fusion(bf16[2,8192,192]{1,2,0:T(8,128)(2,1)S(1)} %bitcast.105, f32[256]{0:T(256)S(1)} %fusion.136, f32[256,8192]{1,0:T(8,128)S(1)} %get-tuple-element.77, f32[256]{0:T(256)S(1)} %get-tuple-element.76, pred[8192]{0:T(1024)(128)(4,1)S(1)} %get-tuple-element.120, ...), kind=kOutput, calls=%fused_computation.315 | convolution fusion | flops 333463296 | bytes 9718784 | tf_op jit(solution)/shard_map/dot_general | solution.py:131
  217.4 5.8 all-reduce.3
  225.8 36.1 %all-reduce.12.cloned.1.call-done = bf16[256,768]{1,0:T(8,128)(2,1)} async-done(((bf16[256,768]{1,0:T(8,128)(2,1)}), bf16[256,768]{1,0:T(8,128)(2,1)}) %all-reduce.12.cloned.1.call-update) | async-done | bytes 393232 | tf_op jit(solution)/shard_map/psum | solution.py:139
  263.2 2.3 fusion.139
  265.6 6.9 all-reduce.2
  273.8 2.9 multiply_reduce_fusion.3
  276.7 6.4 all-reduce.1
  283.0 2.0 fusion.68
  285.0 2.7 convolution_convert_fusion.6
  290.3 35.5 %all-reduce.14.cloned.1.call-done = bf16[256,768]{1,0:T(8,128)(2,1)} async-done(((bf16[256,768]{1,0:T(8,128)(2,1)}), bf16[256,768]{1,0:T(8,128)(2,1)}) %all-reduce.14.cloned.1.call-update) | async-done | bytes 393232 | tf_op jit(solution)/shard_map/psum | solution.py:173
  325.8 2.1 fusion.55
  331.4 6.3 all-reduce
  338.7 17.4 %multiply_reduce_fusion = (f32[256]{0:T(256)}, f32[256,8192]{1,0:T(8,128)S(1)}, f32[256,8192]{1,0:T(8,128)}) fusion(f32[256,8192]{1,0:T(8,128)} %copy-done.13, f32[256]{0:T(256)} %log_add_fusion, pred[8192]{0:T(1024)(128)(4,1)S(1)} %copy-done.45, pred[256]{0:T(512)(128)(4,1)} %copy-done.91, s32[8192]{0:T(1024)S(1)} %get-tuple-element.108, ...), kind=kOutput, calls=%fused_computation.40 | convolution fusion | flops 333446912 | bytes 26462208 | tf_op jit(solution)/shard_map/qe,ke->qk/dot_general | solution.py:207
  356.0 2.3 convolution_convert_fusion
  359.6 7.6 multiply_convert_fusion
  367.2 2.6 fusion.2
  369.8 17.6 %multiply_reduce_fusion.1 = (f32[256]{0:T(256)}, f32[256,8192]{1,0:T(8,128)S(1)}, f32[256,8192]{1,0:T(8,128)}) fusion(f32[256,8192]{1,0:T(8,128)} %copy-done.12, f32[256]{0:T(256)} %log_add_fusion.1, pred[8192]{0:T(1024)(128)(4,1)} %copy-done.40, pred[256]{0:T(512)(128)(4,1)} %copy-done.87, s32[8192]{0:T(1024)} %copy-done.29, s32[256]{0:T(256)} %copy-done.51, ...), kind=kOutput, calls=%fused_computation.43 | convolution fusion | flops 333446912 | bytes 26462208 | tf_op jit(solution)/shard_map/qe,ke->qk/dot_general | solution.py:207
  387.4 3.1 convolution_convert_fusion.1
  390.9 7.6 multiply_convert_fusion.1
  398.5 2.6 fusion.1
  401.1 17.6 %multiply_reduce_fusion.2 = (f32[256]{0:T(256)}, f32[256,8192]{1,0:T(8,128)S(1)}, f32[256,8192]{1,0:T(8,128)}) fusion(f32[256,8192]{1,0:T(8,128)} %copy-done.11, f32[256]{0:T(256)} %log_add_fusion.2, pred[8192]{0:T(1024)(128)(4,1)} %copy-done.36, pred[256]{0:T(512)(128)(4,1)} %copy-done.83, s32[8192]{0:T(1024)} %copy-done.29, s32[256]{0:T(256)} %copy-done.51, ...), kind=kOutput, calls=%fused_computation.46 | convolution fusion | flops 333446912 | bytes 26462208 | tf_op jit(solution)/shard_map/qe,ke->qk/dot_general | solution.py:207
  418.8 3.2 convolution_convert_fusion.2
  422.4 7.6 multiply_convert_fusion.2
  431.8 2.3 maximum_bitcast_fusion
  434.6 3.2 pad_maximum_fusion
  440.4 3.6 convolution_convert_fusion.3
  444.0 2.8 fusion.39
  446.8 2.7 fusion.40
  449.6 2.6 fusion.41
  452.2 220.4 %reduce-scatter.2.cloned.1.call-done = bf16[2,256,192]{1,2,0:T(8,128)(2,1)} async-done(((bf16[2,8192,192]{1,2,0:T(8,128)(2,1)}), bf16[2,256,192]{1,2,0:T(8,128)(2,1)}) %reduce-scatter.2.cloned.1.call-update) | async-done | bytes 196624 | tf_op jit(solution)/shard_map/reduce_scatter | solution.py:223
  672.6 2.5 fusion.35
  675.3 2.7 convolution_convert_fusion.4
  679.0 2.4 fusion.34
  681.5 30.4 %all-reduce.18.cloned.1.call-done = (bf16[256,768]{1,0:T(8,128)(2,1)}, bf16[256,768]{1,0:T(8,128)(2,1)}) async-done(((bf16[256,768]{1,0:T(8,128)(2,1)}, bf16[256,768]{1,0:T(8,128)(2,1)}), (bf16[256,768]{1,0:T(8,128)(2,1)}, bf16[256,768]{1,0:T(8,128)(2,1)})) %all-reduce.18.cloned.1.call-update) | async-done | bytes 786448 | tf_op jit(solution)/shard_map/psum | solution.py:153
  714.5 183.5 %all-reduce.4 = (bf16[768]{0:T(1024)(128)(2,1)S(1)}, bf16[768]{0:T(1024)(128)(2,1)S(1)}, bf16[192]{0:T(256)(128)(2,1)S(1)}, bf16[192]{0:T(256)(128)(2,1)S(1)}, b...) all-reduce(bf16[768]{0:T(1024)(128)(2,1)S(1)} %get-tuple-element.19, ...), channel_id=1, replica_groups=mesh['seq'=32,'tensor'=4] {'seq'}, use_global_device_ids=true, to_apply=%region_45.46 | all-reduce | flops 4992 | bytes 19968 | tf_op jit(solution)/shard_map/psum | solution.py:247
  902.8 2.4 fusion.59
  905.2 175.1 %all-reduce.16.cloned.1.call-done = (bf16[3,768,192]{1,2,0:T(8,128)(2,1)}, bf16[192,768]{1,0:T(8,128)(2,1)}, bf16[768,768]{1,0:T(8,128)(2,1)}, bf16[768,768]{1,0:T(8,128)(2,1)}) async-done(((bf16[3,768,192]{1,2,0:T(8,128)(2,1)}, bf16[192,768]{1,0:T(8,128)(2,1)}, bf16[768,768]{1,0:T(8,128)(2,1)}, bf16[768,768]{1,0:T(8,128)(2,1)}), (bf16[3,768,192]{1,2,0:T(8,128)(2,1)}, bf16[192,768]{1,0:T(8,128)(2,1)}, ...) | async-done | bytes 3538960 | tf_op jit(solution)/shard_map/psum | solution.py:243
  1082.2 2.5 convert_element_type.275
  1084.8 2.8 convert_element_type.279
  (284 shorter events, 36.1 us)
Async XLA Ops:
  7.2 266.6 %copy-start = (bf16[768,768]{1,0:T(8,128)(2,1)S(1)}, bf16[768,768]{1,0:T(8,128)(2,1)}, u32[]{:S(2)}) copy-start(bf16[768,768]{1,0:T(8,128)(2,1)} %param.19) | copy-start | bytes 3538948
  7.2 100.1 %all-gather.2.cloned.1.call-start = ((), (), s32[]{:S(2)}) async-start(), calls=%async_computation.1 | async-start | bytes 6488064 | tf_op jit(solution)/shard_map/all_gather | solution.py:115
  11.3 250.6 %all-reduce.12.cloned.1.call-start = ((), (), s32[]{:S(2)}) async-start(), calls=%async_computation.2 | async-start | bytes 786432 | tf_op jit(solution)/shard_map/psum | solution.py:139
  12.2 182.0 %copy-start.87 = (pred[256]{0:T(512)(128)(4,1)}, pred[256]{0:T(512)(128)(4,1)S(1)}, u32[]{:S(2)}) copy-start(pred[256]{0:T(512)(128)(4,1)S(1)} %get-tuple-element.100) | copy-start | bytes 772
  12.2 182.0 %copy-start.88 = (pred[256]{0:T(512)(128)(4,1)}, pred[256]{0:T(512)(128)(4,1)S(1)}, u32[]{:S(2)}) copy-start(pred[256]{0:T(512)(128)(4,1)S(1)} %get-tuple-element.101) | copy-start | bytes 772
  12.3 193.3 %copy-start.83 = (pred[256]{0:T(512)(128)(4,1)}, pred[256]{0:T(512)(128)(4,1)S(1)}, u32[]{:S(2)}) copy-start(pred[256]{0:T(512)(128)(4,1)S(1)} %get-tuple-element.104) | copy-start | bytes 772
  12.3 193.3 %copy-start.84 = (pred[256]{0:T(512)(128)(4,1)}, pred[256]{0:T(512)(128)(4,1)S(1)}, u32[]{:S(2)}) copy-start(pred[256]{0:T(512)(128)(4,1)S(1)} %get-tuple-element.105) | copy-start | bytes 772
  12.3 193.3 %copy-start.85 = (pred[256]{0:T(512)(128)(4,1)}, pred[256]{0:T(512)(128)(4,1)S(1)}, u32[]{:S(2)}) copy-start(pred[256]{0:T(512)(128)(4,1)S(1)} %get-tuple-element.106) | copy-start | bytes 772
  12.3 193.3 %copy-start.86 = (pred[256]{0:T(512)(128)(4,1)}, pred[256]{0:T(512)(128)(4,1)S(1)}, u32[]{:S(2)}) copy-start(pred[256]{0:T(512)(128)(4,1)S(1)} %get-tuple-element.107) | copy-start | bytes 772
  12.4 181.9 %copy-start.89 = (pred[256]{0:T(512)(128)(4,1)}, pred[256]{0:T(512)(128)(4,1)S(1)}, u32[]{:S(2)}) copy-start(pred[256]{0:T(512)(128)(4,1)S(1)} %get-tuple-element.102) | copy-start | bytes 772
  12.4 181.9 %copy-start.90 = (pred[256]{0:T(512)(128)(4,1)}, pred[256]{0:T(512)(128)(4,1)S(1)}, u32[]{:S(2)}) copy-start(pred[256]{0:T(512)(128)(4,1)S(1)} %get-tuple-element.103) | copy-start | bytes 772
  13.0 192.6 %copy-start.51 = (s32[256]{0:T(256)}, s32[256]{0:T(256)S(1)}, u32[]{:S(2)}) copy-start(s32[256]{0:T(256)S(1)} %get-tuple-element.90) | copy-start | bytes 3076
  13.0 192.6 %copy-start.53 = (s32[256]{0:T(256)}, s32[256]{0:T(256)S(1)}, u32[]{:S(2)}) copy-start(s32[256]{0:T(256)S(1)} %get-tuple-element.91) | copy-start | bytes 3076
  13.0 192.6 %copy-start.54 = (s32[256]{0:T(256)}, s32[256]{0:T(256)S(1)}, u32[]{:S(2)}) copy-start(s32[256]{0:T(256)S(1)} %get-tuple-element.92) | copy-start | bytes 3076
  13.0 192.6 %copy-start.55 = (s32[256]{0:T(256)}, s32[256]{0:T(256)S(1)}, u32[]{:S(2)}) copy-start(s32[256]{0:T(256)S(1)} %get-tuple-element.93) | copy-start | bytes 3076
  13.1 192.6 %copy-start.56 = (s32[256]{0:T(256)}, s32[256]{0:T(256)S(1)}, u32[]{:S(2)}) copy-start(s32[256]{0:T(256)S(1)} %get-tuple-element.94) | copy-start | bytes 3076
  13.1 192.6 %copy-start.57 = (s32[256]{0:T(256)}, s32[256]{0:T(256)S(1)}, u32[]{:S(2)}) copy-start(s32[256]{0:T(256)S(1)} %get-tuple-element.95) | copy-start | bytes 3076
  13.2 181.1 %copy-start.38 = (pred[8192]{0:T(1024)(128)(4,1)}, pred[8192]{0:T(1024)(128)(4,1)S(1)}, u32[]{:S(2)}) copy-start(pred[8192]{0:T(1024)(128)(4,1)S(1)} %get-tuple-element.118) | copy-start | bytes 24580
  13.2 181.1 %copy-start.39 = (pred[8192]{0:T(1024)(128)(4,1)}, pred[8192]{0:T(1024)(128)(4,1)S(1)}, u32[]{:S(2)}) copy-start(pred[8192]{0:T(1024)(128)(4,1)S(1)} %get-tuple-element.119) | copy-start | bytes 24580
  13.2 192.5 %copy-start.34 = (pred[8192]{0:T(1024)(128)(4,1)}, pred[8192]{0:T(1024)(128)(4,1)S(1)}, u32[]{:S(2)}) copy-start(pred[8192]{0:T(1024)(128)(4,1)S(1)} %get-tuple-element.122) | copy-start | bytes 24580
  13.2 192.5 %copy-start.35 = (pred[8192]{0:T(1024)(128)(4,1)}, pred[8192]{0:T(1024)(128)(4,1)S(1)}, u32[]{:S(2)}) copy-start(pred[8192]{0:T(1024)(128)(4,1)S(1)} %get-tuple-element.123) | copy-start | bytes 24580
  13.3 192.4 %copy-start.36 = (pred[8192]{0:T(1024)(128)(4,1)}, pred[8192]{0:T(1024)(128)(4,1)S(1)}, u32[]{:S(2)}) copy-start(pred[8192]{0:T(1024)(128)(4,1)S(1)} %get-tuple-element.120) | copy-start | bytes 24580
  13.3 192.4 %copy-start.37 = (pred[8192]{0:T(1024)(128)(4,1)}, pred[8192]{0:T(1024)(128)(4,1)S(1)}, u32[]{:S(2)}) copy-start(pred[8192]{0:T(1024)(128)(4,1)S(1)} %get-tuple-element.121) | copy-start | bytes 24580
  13.3 180.9 %copy-start.40 = (pred[8192]{0:T(1024)(128)(4,1)}, pred[8192]{0:T(1024)(128)(4,1)S(1)}, u32[]{:S(2)}) copy-start(pred[8192]{0:T(1024)(128)(4,1)S(1)} %get-tuple-element.116) | copy-start | bytes 24580
  13.3 180.9 %copy-start.41 = (pred[8192]{0:T(1024)(128)(4,1)}, pred[8192]{0:T(1024)(128)(4,1)S(1)}, u32[]{:S(2)}) copy-start(pred[8192]{0:T(1024)(128)(4,1)S(1)} %get-tuple-element.117) | copy-start | bytes 24580
  13.4 325.1 %copy-start.27 = (s32[8192]{0:T(1024)}, s32[8192]{0:T(1024)S(1)}, u32[]{:S(2)}) copy-start(s32[8192]{0:T(1024)S(1)} %get-tuple-element.110) | copy-start | bytes 98308
  13.5 325.1 %copy-start.28 = (s32[8192]{0:T(1024)}, s32[8192]{0:T(1024)S(1)}, u32[]{:S(2)}) copy-start(s32[8192]{0:T(1024)S(1)} %get-tuple-element.111) | copy-start | bytes 98308
  13.5 325.1 %copy-start.29 = (s32[8192]{0:T(1024)}, s32[8192]{0:T(1024)S(1)}, u32[]{:S(2)}) copy-start(s32[8192]{0:T(1024)S(1)} %get-tuple-element.108) | copy-start | bytes 98308
  13.5 325.1 %copy-start.30 = (s32[8192]{0:T(1024)}, s32[8192]{0:T(1024)S(1)}, u32[]{:S(2)}) copy-start(s32[8192]{0:T(1024)S(1)} %get-tuple-element.109) | copy-start | bytes 98308
  224.4 101.4 %all-reduce.14.cloned.1.call-start = ((), (), s32[]{:S(2)}) async-start(), calls=%async_computation.3 | async-start | bytes 786432 | tf_op jit(solution)/shard_map/psum | solution.py:173
  287.7 384.9 %reduce-scatter.2.cloned.1.call-start = ((), (), s32[]{:S(2)}) async-start(), calls=%async_computation.4 | async-start | bytes 6488064 | tf_op jit(solution)/shard_map/reduce_scatter | solution.py:223
  437.8 274.2 %all-reduce.18.cloned.1.call-start = ((), (), s32[]{:S(2)}) async-start(), calls=%async_computation.6 | async-start | bytes 1572864 | tf_op jit(solution)/shard_map/psum | solution.py:153
  446.7 228.5 %copy-start.15 = (bf16[256,768]{1,0:T(8,128)(2,1)S(1)}, bf16[256,768]{1,0:T(8,128)(2,1)}, u32[]{:S(2)}) copy-start(bf16[256,768]{1,0:T(8,128)(2,1)} %all-reduce.12.cloned.1.call-done) | copy-start | bytes 1179652
  446.7 228.5 %copy-start.49 = (f32[768]{0:T(1024)S(1)}, f32[768]{0:T(1024)}, u32[]{:S(2)}) copy-start(f32[768]{0:T(1024)} %param.24) | copy-start | bytes 9220
  446.8 228.5 %copy-start.67 = (f32[256]{0:T(256)S(1)}, f32[256]{0:T(256)}, u32[]{:S(2)}) copy-start(f32[256]{0:T(256)} %copy-done.66) | copy-start | bytes 3076
  446.8 228.5 %copy-start.69 = (f32[256]{0:T(256)S(1)}, f32[256]{0:T(256)}, u32[]{:S(2)}) copy-start(f32[256]{0:T(256)} %copy-done.68) | copy-start | bytes 3076
  446.8 228.5 %copy-start.102 = (f32[768]{0:T(1024)S(1)}, f32[768]{0:T(1024)}, u32[]{:S(2)}) copy-start(f32[768]{0:T(1024)} %param.25) | copy-start | bytes 9220
  449.5 228.5 %copy-start.24 = (f32[256,64]{0,1:T(8,128)S(1)}, f32[256,64]{0,1:T(8,128)}, u32[]{:S(2)}) copy-start(f32[256,64]{0,1:T(8,128)} %copy-done.23) | copy-start | bytes 196612
  449.5 228.5 %copy-start.59 = (f32[256]{0:T(256)S(1)}, f32[256]{0:T(256)}, u32[]{:S(2)}) copy-start(f32[256]{0:T(256)} %copy-done.58) | copy-start | bytes 3076
  449.5 228.5 %copy-start.61 = (f32[256]{0:T(256)S(1)}, f32[256]{0:T(256)}, u32[]{:S(2)}) copy-start(f32[256]{0:T(256)} %copy-done.60) | copy-start | bytes 3076
  449.5 228.5 %copy-start.71 = (f32[192]{0:T(256)S(1)}, f32[192]{0:T(256)}, u32[]{:S(2)}) copy-start(f32[192]{0:T(256)} %param.22) | copy-start | bytes 2308
  449.5 228.5 %copy-start.99 = (f32[192]{0:T(256)S(1)}, f32[192]{0:T(256)}, u32[]{:S(2)}) copy-start(f32[192]{0:T(256)} %param.23) | copy-start | bytes 2308
  449.5 229.5 %copy-start.50 = (f32[768]{0:T(1024)S(1)}, f32[768]{0:T(1024)}, u32[]{:S(2)}) copy-start(f32[768]{0:T(1024)} %param.20) | copy-start | bytes 9220
  449.5 229.5 %copy-start.63 = (f32[256]{0:T(256)S(1)}, f32[256]{0:T(256)}, u32[]{:S(2)}) copy-start(f32[256]{0:T(256)} %copy-done.62) | copy-start | bytes 3076
  449.5 229.5 %copy-start.65 = (f32[256]{0:T(256)S(1)}, f32[256]{0:T(256)}, u32[]{:S(2)}) copy-start(f32[256]{0:T(256)} %copy-done.64) | copy-start | bytes 3076
  449.6 229.5 %copy-start.103 = (f32[768]{0:T(1024)S(1)}, f32[768]{0:T(1024)}, u32[]{:S(2)}) copy-start(f32[768]{0:T(1024)} %param.21) | copy-start | bytes 9220
  452.2 229.2 %copy-start.19 = (bf16[256,768]{1,0:T(8,128)(2,1)S(1)}, bf16[256,768]{1,0:T(8,128)(2,1)}, u32[]{:S(2)}) copy-start(bf16[256,768]{1,0:T(8,128)(2,1)} %all-reduce.14.cloned.1.call-done) | copy-start | bytes 1179652
  675.2 405.1 %all-reduce.16.cloned.1.call-start = ((), (), s32[]{:S(2)}) async-start(), calls=%async_computation.5 | async-start | bytes 7077888 | tf_op jit(solution)/shard_map/psum | solution.py:243
  (64 other events, 2640.0 us)
Sparse Core Ops, SparseCore 0:
  11.4 95.8 all-gather.1
  224.5 37.3 all-reduce.11
  287.8 37.9 all-reduce.13
  437.9 234.6 reduce-scatter.1
  675.6 36.2 all-reduce.17
  715.1 365.1 all-reduce.15
where the time goes:
time: 1110 us; the launch traced here: 1100 us
  waiting for transfers between devices  591 us (53%)
  blocking collectives  209 us (19%)
  matrix products  169 us (15%)
  other arithmetic  104 us (9%)
  between operations  16.7 us (2%)
    reduce_scatter x1, waiting for transfers between devices, per_device(): lax.psum_scatter(pair_terms.astype(jnp.bfloat16), 'seq', scatter_dimensio...  220 us
    psum x1, blocking collectives, per_device(): lax.psum(in_gain_grad.astype(jnp.bfloat16), 'seq').astype(jnp.float32)  184 us
    psum x1, waiting for transfers between devices, per_device(): lax.psum(head_grad.astype(jnp.bfloat16), 'seq').astype(jnp.float32)  175 us
    all_gather x1, waiting for transfers between devices, per_device(): gathered_pairs = lax.all_gather(projected[1:], 'seq', axis=1, tiled=True)  93.8 us
    dot_general x3, matrix products, per_device(): jnp.einsum('qe,ke->qk', head_grad_rows, value_block, preferred_element_ty...  52.6 us
    reduce_sum x3, other arithmetic, per_device(): totals = jnp.sum(weighted, 1, keepdims=True)  42.8 us
    psum x1, waiting for transfers between devices, per_device(): lax.psum(jnp.dot(mix_low, out_weight, preferred_element_type=jnp.float32)...  36.1 us
    psum x1, waiting for transfers between devices, per_device(): lax.psum(jnp.einsum('tf,df->td', pre_grad, up_weight, preferred_element_t...  35.5 us
  transfers between devices with their start and end apart: 6, of which 6 were waited for; matrix products, arithmetic and copies ran while one was open for 3% of the time, Pallas kernels for 0%

commit v1 on v0

v1 whole, which is shorter than its diff:
```python
import functools

import jax
import jax.numpy as jnp
import numpy as np
from jax import lax
from jax.experimental import pallas as pl
from jax.experimental.pallas import tpu as pltpu
from jax.sharding import Mesh
from jax.sharding import PartitionSpec as P


HDIM = 64
HEADS_HERE = 3
TOK = 256
PLANE = 8
SLOTS = 128
EPSILON = 1e-05
NONE = -1e30
NEAR = (1, 2, 4, 6, 12)
MID = (2, 4, 6, 12)
FAR = (4, 6, 12)
F32 = jnp.float32
BF16 = jnp.bfloat16
SEQ = ("z", "yh", "x")
TENSOR = ("yl", "c")
FLIP = [(0, 1), (1, 0)]


def dot(a, b, dims=((1,), (0,))):
    return lax.dot_general(a, b, (dims, ((), ())), preferred_element_type=F32)


def split3(v):
    hi = v.astype(BF16).astype(F32)
    mid = (v - hi).astype(BF16).astype(F32)
    return hi, mid, (v - hi - mid).astype(BF16).astype(F32)


def mid_offsets(head):
    slot = lax.broadcasted_iota(jnp.int32, (1, SLOTS), 1)
    return 2 * slot + lax.rem(head, 2)


def far_offsets(head, base):
    slot = lax.broadcasted_iota(jnp.int32, (1, SLOTS), 1)
    which = lax.rem(slot, 4)
    kind = jnp.where(which == 0, 0, 2 * which + 2)
    first = lax.div(base + 12 - head, 12) - 1
    return 12 * (first + lax.div(slot, 4)) + kind + head - base, kind


def one_hot_rows(offsets):
    rows = lax.broadcasted_iota(jnp.int32, (TOK, SLOTS), 0)
    return (rows == offsets).astype(F32).astype(BF16)


def count_table(kind, usable, dilations):
    row = lax.broadcasted_iota(jnp.int32, (16, kind.shape[1]), 0)
    count = jnp.zeros(row.shape, F32)
    for step in dilations:
        count += jnp.where((lax.rem(row, step) == 0) & (lax.rem(kind, step) == 0), 1.0, 0.0)
    live = (count > 0) & usable
    log_count = jnp.log(jnp.maximum(count, 1.0))
    hi = log_count.astype(BF16).astype(F32)
    return jnp.where(live, hi, NONE), jnp.where(live, log_count - hi, 0.0)


def query_rows(head, base, plane, q, qa, qb, qc, lo):
    own_kind = lax.rem(base - head + 12 + lax.broadcasted_iota(jnp.int32, (1, TOK), 1), 12)
    mid_at = mid_offsets(head)
    block = lax.rem(base, 2048)
    parts = [
        (q, own_kind, own_kind >= 0, NEAR),
        (qa, lax.rem(base + 2048 + mid_at - head + 12, 12), (mid_at >= 0) & (lax.rem(plane, 2) == 0), MID),
    ]
    for visitor, origin in ((qb, plane + 2), (qc, 3 - plane)):
        at, kind = far_offsets(head, origin * 2048 + block)
        parts.append((visitor, kind, (at >= 0) & (at < TOK) & (plane < 2), FAR))
    columns = []
    for ref, kind, usable, dilations in parts:
        hi, low = count_table(kind, usable, dilations)
        scaled = ref[lo : lo + HDIM, :].astype(F32) * 0.125
        columns.append(jnp.concatenate([scaled, hi, low, jnp.zeros((32, scaled.shape[1]), F32)], 0))
    return columns


def key_columns(head, key_base, kv, lo):
    kind = lax.rem(key_base - head + 12 + lax.broadcasted_iota(jnp.int32, (16, TOK), 1), 12)
    hot = (kind == lax.broadcasted_iota(jnp.int32, (16, TOK), 0)).astype(F32).astype(BF16)
    return jnp.concatenate([kv[lo : lo + HDIM, :], hot, hot, jnp.ones((32, TOK), BF16)], 0)


def value_columns(kv, lo):
    return jnp.concatenate([kv[192 + lo : 192 + lo + HDIM, :], jnp.ones((HDIM, TOK), BF16)], 0)


def diagonal_mask(base, valid):
    rows = lax.broadcasted_iota(jnp.int32, (TOK, TOK), 0)
    cols = lax.broadcasted_iota(jnp.int32, (TOK, TOK), 1)
    return (cols <= rows) & (cols + base < valid)


def forward_kernel(sc, q, qa, qb, qc, *refs):
    kvs = refs[:PLANE]
    o_near, st_near, pay_a, pay_b, pay_c, loc = refs[PLANE : PLANE + 6]
    left, s_near, s_far, m_near, m_far, acc_near, acc_far = refs[PLANE + 6 :]
    head0, base, place, plane, valid = (sc[i] for i in range(5))
    lane = lax.broadcasted_iota(jnp.int32, (1, 128), 1)
    st_near[...] = jnp.zeros((TOK, 128), F32)
    loc[...] = jnp.zeros((384, 128), F32)
    extra = [jnp.where(lane[:, :64] == 9, 1.0, jnp.zeros((SLOTS, 64), F32)) for _ in range(3)]
    for h in range(HEADS_HERE):
        lo = h * HDIM
        head = head0 + h
        columns = query_rows(head, base, plane, q, qa, qb, qc, lo)
        at = 0
        for part in columns:
            left[at : at + part.shape[1], :] = part.T.astype(BF16)
            at += part.shape[1]
        m_near[...] = jnp.full((TOK, 128), NONE * 2, F32)
        m_far[...] = jnp.full((384, 128), NONE * 2, F32)
        acc_near[...] = jnp.zeros((TOK, 128), F32)
        acc_far[...] = jnp.zeros((384, 128), F32)
        for k in range(PLANE):
            block = lax.rem(place - k + PLANE, PLANE)
            right = key_columns(head, plane * 2048 + block * TOK, kvs[k], lo)

            @pl.when(k <= place)
            def _():
                s = dot(left[0:TOK, :], right)
                if k == 0:
                    s = jnp.where(diagonal_mask(base, valid), s, NONE)
                s_near[k] = s
                m_near[...] = jnp.maximum(m_near[...], jnp.maximum(s[:, :128], s[:, 128:]))

            @pl.when(plane < 3)
            def _():
                s = dot(left[TOK:, :], right)
                s_far[k] = s
                m_far[...] = jnp.maximum(m_far[...], jnp.maximum(s[:, :128], s[:, 128:]))

        top_near = jnp.max(m_near[...], 1, keepdims=True)
        top_far = jnp.max(m_far[...], 1, keepdims=True)
        for k in range(PLANE):
            values = value_columns(kvs[k], lo)

            @pl.when(k <= place)
            def _():
                w = jnp.exp(s_near[k] - top_near).astype(BF16)
                acc_near[...] += dot(w, values, ((1,), (1,)))

            @pl.when(plane < 3)
            def _():
                w = jnp.exp(s_far[k] - top_far).astype(BF16)
                acc_far[...] += dot(w, values, ((1,), (1,)))

        total = acc_near[:, 64:65]
        o_near[:, lo : lo + HDIM] = acc_near[:, :64] / total
        st_near[...] = jnp.where(lane == h, top_near + jnp.log(total), st_near[...])
        total = jnp.maximum(acc_far[:, 64:65], 1e-30)
        out = (acc_far[:, :64] / total).astype(BF16)
        lse = jnp.maximum(top_far + jnp.log(total), NONE)
        loc[...] = jnp.where(lane == h, lse, loc[...])
        terms = split3(lse)
        for i, pay in enumerate((pay_a, pay_b, pay_c)):
            rows = slice(i * SLOTS, (i + 1) * SLOTS)
            pay[:, lo : lo + HDIM] = out[rows, :]
            for j, term in enumerate(terms):
                extra[i] = jnp.where(lane[:, :64] == 3 * h + j, term[rows, :], extra[i])
    for i, pay in enumerate((pay_a, pay_b, pay_c)):
        pay[:, 192:256] = extra[i].astype(BF16)


def combine_kernel(sc, o_near, st_near, ra, rb, rc, o_all, mixed, st_all):
    head0, base = sc[0], sc[1]
    lane = lax.broadcasted_iota(jnp.int32, (1, 128), 1)
    st = jnp.zeros((TOK, 128), F32)
    for h in range(HEADS_HERE):
        lo = h * HDIM
        head = head0 + h
        pick_mid = one_hot_rows(mid_offsets(head))
        pick_far = one_hot_rows(far_offsets(head, base)[0])
        own = st_near[:, h : h + 1]
        outs, logs = [o_near[:, lo : lo + HDIM]], [own]
        for pay, pick in ((ra, pick_mid), (rb, pick_far), (rc, pick_far)):
            wide = dot(pick, pay[...])
            log = wide[:, 192 + 3 * h : 193 + 3 * h] + wide[:, 193 + 3 * h : 194 + 3 * h] + wide[:, 194 + 3 * h : 195 + 3 * h]
            outs.append(wide[:, lo : lo + HDIM])
            logs.append(jnp.where(wide[:, 201:202] > 0.5, log, NONE))
        top = functools.reduce(jnp.maximum, logs)
        weights = [jnp.exp(v - top) for v in logs]
        total = sum(weights)
        mixed_h = sum(w * o for w, o in zip(weights, outs)) / total
        o_all[:, lo : lo + HDIM] = mixed_h
        mixed[:, lo : lo + HDIM] = mixed_h.astype(BF16)
        st = jnp.where(lane == h, top + jnp.log(total), st)
        for i in range(3):
            st = jnp.where(lane == 3 + 3 * i + h, weights[i + 1] / total, st)
    st_all[...] = st


def prepare_kernel(sc, grad, o_all, st_all, st_near, pay_a, pay_b, pay_c):
    head0, base = sc[0], sc[1]
    lane = lax.broadcasted_iota(jnp.int32, (1, 128), 1)
    st = jnp.zeros((TOK, 128), F32)
    pays = [jnp.zeros((SLOTS, 256), F32) for _ in range(3)]
    wide_lane = lax.broadcasted_iota(jnp.int32, (1, 256), 1)
    full = grad[...].astype(F32)
    product = full * o_all[...]
    full = jnp.concatenate([full, jnp.zeros((TOK, 64), F32)], 1)
    for h in range(HEADS_HERE):
        lo = h * HDIM
        head = head0 + h
        centre = jnp.sum(product[:, lo : lo + HDIM], 1, keepdims=True)
        st = jnp.where(lane == h, st_all[:, h : h + 1], st)
        st = jnp.where(lane == 3 + h, centre, st)
        pick_mid = one_hot_rows(mid_offsets(head))
        pick_far = one_hot_rows(far_offsets(head, base)[0])
        mine = jnp.where((wide_lane >= lo) & (wide_lane < lo + HDIM), full, 0.0)
        for i, pick in enumerate((pick_mid, pick_far, pick_far)):
            share = st_all[:, 3 + 3 * i + h : 4 + 3 * i + h]
            wide = mine * share
            for j, term in enumerate(split3(centre * share)):
                wide = jnp.where(wide_lane == 192 + 3 * h + j, term, wide)
            pays[i] += dot(pick, wide.astype(BF16), ((0,), (0,)))
    st_near[...] = st
    for pay, value in zip((pay_a, pay_b, pay_c), pays):
        pay[...] = value.astype(BF16)


def backward_kernel(sc, q, qa, qb, qc, grad, st_near, pay_a, pay_b, pay_c, loc, *refs):
    kvs = refs[:PLANE]
    dq_near, dq_a, dq_b, dq_c = refs[PLANE : PLANE + 4]
    dkvs = refs[PLANE + 4 : 2 * PLANE + 4]
    left, grad_left, turned, acc_q, acc_kv = refs[2 * PLANE + 4 :]
    head0, base, place, plane, valid = (sc[i] for i in range(5))
    lane = lax.broadcasted_iota(jnp.int32, (1, 128), 1)
    for pay in (dq_a, dq_b, dq_c):
        pay[...] = jnp.zeros((SLOTS, 256), BF16)
    for h in range(HEADS_HERE):
        lo = h * HDIM
        head = head0 + h
        columns = query_rows(head, base, plane, q, qa, qb, qc, lo)
        logs = [st_near[:, h : h + 1]] + [loc[i * SLOTS : (i + 1) * SLOTS, h : h + 1] for i in range(3)]
        grads = [grad[:, lo : lo + HDIM].astype(F32)] + [v[:, lo : lo + HDIM].astype(F32) for v in (pay_a, pay_b, pay_c)]
        centres = [st_near[:, 3 + h : 4 + h]]
        for v in (pay_a, pay_b, pay_c):
            e = v[:, 192:256].astype(F32)
            centres.append(e[:, 3 * h : 3 * h + 1] + e[:, 3 * h + 1 : 3 * h + 2] + e[:, 3 * h + 2 : 3 * h + 3])
        at = 0
        for part, log, g, centre in zip(columns, logs, grads, centres):
            n = part.shape[1]
            rows = slice(at, at + n)
            natural = part.T
            for j, term in enumerate(split3(jnp.where(log > NONE * 0.1, -log, 0.0))):
                natural = jnp.where(lane == 96 + j, term, natural)
            left[rows, :] = natural.astype(BF16)
            natural = jnp.concatenate([g, jnp.zeros((n, 64), F32)], 1)
            for j, term in enumerate(split3(-centre)):
                natural = jnp.where(lane == 64 + j, term, natural)
            grad_left[rows, :] = natural.astype(BF16)
            turned[0:64, rows] = part[0:64, :].astype(BF16)
            turned[64:128, rows] = natural.T[0:64, :].astype(BF16)
            at += n
        acc_q[...] = jnp.zeros((640, HDIM), F32)
        for k in range(PLANE):
            block = lax.rem(place - k + PLANE, PLANE)
            right = key_columns(head, plane * 2048 + block * TOK, kvs[k], lo)
            values = value_columns(kvs[k], lo)
            acc_kv[...] = jnp.zeros((128, TOK), F32)

            def part(rows, masked):
                s = dot(left[rows, :], right)
                if masked:
                    s = jnp.where(diagonal_mask(base, valid), s, NONE)
                w = jnp.exp(s)
                ds = (w * dot(grad_left[rows, :], values)).astype(BF16)
                acc_q[rows, :] += dot(ds, kvs[k][lo : lo + HDIM, :], ((1,), (1,)))
                acc_kv[0:64, :] += dot(turned[0:64, rows], ds)
                acc_kv[64:128, :] += dot(turned[64:128, rows], w.astype(BF16))

            @pl.when(k <= place)
            def _():
                part(slice(0, TOK), k == 0)

            @pl.when(plane < 3)
            def _():
                part(slice(TOK, 640), False)

            dkvs[k][lo : lo + HDIM, :] = acc_kv[0:64, :].astype(BF16)
            dkvs[k][192 + lo : 192 + lo + HDIM, :] = acc_kv[64:128, :].astype(BF16)
        dq_near[:, lo : lo + HDIM] = acc_q[0:TOK, :] * 0.125
        for i, pay in enumerate((dq_a, dq_b, dq_c)):
            pay[:, lo : lo + HDIM] = (acc_q[TOK + i * SLOTS : TOK + (i + 1) * SLOTS, :] * 0.125).astype(BF16)


def collect_kernel(sc, dq_near, ra, rb, rc, dq):
    head0, base = sc[0], sc[1]
    for h in range(HEADS_HERE):
        lo = h * HDIM
        head = head0 + h
        pick_mid = one_hot_rows(mid_offsets(head))
        pick_far = one_hot_rows(far_offsets(head, base)[0])
        far = (rb[...].astype(F32) + rc[...].astype(F32)).astype(BF16)
        wide = dot(pick_mid, ra[...]) + dot(pick_far, far)
        dq[:, lo : lo + HDIM] = (dq_near[:, lo : lo + HDIM] + wide[:, lo : lo + HDIM]).astype(BF16)


def call(kernel, out_shapes, scratch=()):
    def run(sc, *args):
        return pl.pallas_call(
            kernel,
            out_shape=[jax.ShapeDtypeStruct(s, d) for s, d in out_shapes],
            in_specs=[pl.BlockSpec(memory_space=pltpu.SMEM)] + [pl.BlockSpec(memory_space=pltpu.VMEM)] * len(args),
            out_specs=[pl.BlockSpec(memory_space=pltpu.VMEM)] * len(out_shapes),
            scratch_shapes=list(scratch),
            compiler_params=pltpu.CompilerParams(vmem_limit_bytes=48 * 1024 * 1024),
        )(sc, *args)

    return run


def norm_rows(v, gain, shift):
    mean = jnp.sum(v, 1, keepdims=True) / v.shape[1]
    spread = jnp.sum(v * v, 1, keepdims=True) / v.shape[1] - mean * mean
    scale = lax.rsqrt(spread + EPSILON)
    unit = (v - mean) * scale
    return unit * gain + shift, unit, scale


def norm_rows_back(grad, unit, scale, gain):
    q = grad * gain
    n = grad.shape[1]
    return scale * (q - jnp.sum(q, 1, keepdims=True) / n - unit * jnp.sum(q * unit, 1, keepdims=True) / n)


PAIR_A = [(0, 1), (1, 0), (2, 3), (3, 2)]
PAIR_B = [(0, 3), (3, 0), (1, 2), (2, 1)]
ORDERS = (
    ("xa", "xb", "za", "zb", "y"),
    ("xb", "xa", "zb", "za", "y"),
    ("za", "zb", "xa", "xb", "y"),
    ("zb", "za", "xb", "xa", "y"),
)


def halving_steps():
    x, z, y = lax.axis_index("x"), lax.axis_index("z"), lax.axis_index("yh")

    def side_a(i):
        return jnp.where((i == 0) | (i == 3), 0, 1)

    def side_b(i):
        return jnp.where(i < 2, 0, 1)

    return {
        "xa": ("x", PAIR_A, side_a(x)),
        "xb": ("x", PAIR_B, side_b(x)),
        "za": ("z", PAIR_A, side_a(z)),
        "zb": ("z", PAIR_B, side_b(z)),
        "y": ("yh", FLIP, y),
    }


def sum_over_seq(v):
    steps = halving_steps()
    parts = jnp.split(v, 4)
    for i in range(5):
        for j in range(4):
            axis, perm, side = steps[ORDERS[j][i]]
            n = parts[j].shape[0] // 2
            keep = lax.dynamic_slice_in_dim(parts[j], side * n, n, 0)
            send = lax.dynamic_slice_in_dim(parts[j], (1 - side) * n, n, 0)
            parts[j] = keep + lax.ppermute(send, axis, perm)
    for i in range(4, -1, -1):
        for j in range(4):
            axis, perm, side = steps[ORDERS[j][i]]
            other = lax.ppermute(parts[j], axis, perm)
            parts[j] = jnp.where(
                side == 0, jnp.concatenate([parts[j], other]), jnp.concatenate([other, parts[j]])
            )
    return jnp.concatenate(parts)


def sum_over_tensor(v):
    core = lax.axis_index("c")
    n = v.shape[0] // 2
    keep = lax.dynamic_slice_in_dim(v, core * n, n, 0)
    send = lax.dynamic_slice_in_dim(v, (1 - core) * n, n, 0)
    half = keep + lax.ppermute(send, "c", FLIP)
    half = half + lax.ppermute(half, "yl", FLIP)
    other = lax.ppermute(half, "c", FLIP)
    return jnp.where(core == 0, jnp.concatenate([half, other]), jnp.concatenate([other, half]))


def sum_small_over_tensor(v):
    v = v + lax.ppermute(v, "c", FLIP)
    return v + lax.ppermute(v, "yl", FLIP)


def gather_over_tensor(v):
    across = lax.ppermute(v, "yl", FLIP)
    beside = lax.ppermute(v, "c", FLIP)
    both = lax.ppermute(across, "c", FLIP)
    core, low = lax.axis_index("c"), lax.axis_index("yl")
    here = [jnp.where(core == 0, v, beside), jnp.where(core == 0, beside, v)]
    there = [jnp.where(core == 0, across, both), jnp.where(core == 0, both, across)]
    return [jnp.where(low == 0, a, b) for a, b in zip(here + there, there + here)]


MID_GO = [(1, 0), (3, 2)]
B_GO = [(2, 0), (3, 1)]
C_GO = [(3, 0), (2, 1)]


def back(perm):
    return [(b, a) for a, b in perm]


def smooth(v):
    return jax.nn.gelu(v, approximate=True)


def per_device(
    inputs,
    head_weights,
    out_weight,
    up_weight,
    down_weight,
    in_gain,
    in_shift,
    mix_gain,
    mix_shift,
    mid_gain,
    mid_shift,
    inner_gain,
    inner_shift,
    valid_length,
    cotangent,
):
    z, yh, x = (lax.axis_index(a) for a in SEQ)
    place = yh * 4 + x
    tensor = lax.axis_index("yl") * 2 + lax.axis_index("c")
    head0 = tensor * HEADS_HERE
    base = (z * PLANE + place) * TOK
    valid = valid_length[0]
    sc = jnp.stack([head0, base, place, z, valid]).astype(jnp.int32)
    row_valid = (base + jnp.arange(TOK, dtype=jnp.int32) < valid)[:, None]

    vectors = jnp.stack(split3(mix_gain) + split3(mix_shift)).astype(BF16)
    packed = jnp.concatenate([out_weight.T, vectors, jnp.zeros((10, 192), BF16)], 0)
    packed = lax.all_gather(packed, TENSOR, axis=0)
    out_full = packed[:, :768].transpose(1, 0, 2).reshape(768, 768)
    gain_full = jnp.sum(packed[:, 768:771].astype(F32), 1).reshape(768)
    shift_full = jnp.sum(packed[:, 771:774].astype(F32), 1).reshape(768)

    source = inputs.astype(F32)
    normed, in_unit, in_scale = norm_rows(source, in_gain, in_shift)
    normed_low = normed.astype(BF16)
    projected = jnp.einsum("td,cde->cet", normed_low, head_weights, preferred_element_type=F32).astype(BF16)
    queries = projected[0]
    pairs = projected[1:].reshape(384, TOK)

    kvs = [pairs] + [
        lax.ppermute(pairs, ("yh", "x"), [(i, (i + k) % PLANE) for i in range(PLANE)]) for k in range(1, PLANE)
    ]
    pick_mid = jnp.stack([one_hot_rows(mid_offsets(head0 + h)) for h in range(HEADS_HERE)])
    pick_far = jnp.stack([one_hot_rows(far_offsets(head0 + h, base)[0]) for h in range(HEADS_HERE)])
    by_head = queries.reshape(HEADS_HERE, HDIM, TOK)
    q_mid = jnp.einsum("het,htj->hej", by_head, pick_mid, preferred_element_type=F32).astype(BF16).reshape(192, SLOTS)
    q_far = jnp.einsum("het,htj->hej", by_head, pick_far, preferred_element_type=F32).astype(BF16).reshape(192, SLOTS)
    qa = lax.ppermute(q_mid, "z", MID_GO)
    qb = lax.ppermute(q_far, "z", B_GO)
    qc = lax.ppermute(q_far, "z", C_GO)

    o_near, st_near, pay_a, pay_b, pay_c, loc = call(
        forward_kernel,
        [((TOK, 192), F32), ((TOK, 128), F32)] + [((SLOTS, 256), BF16)] * 3 + [((384, 128), F32)],
        [
            pltpu.VMEM((640, 128), BF16),
            pltpu.VMEM((PLANE, TOK, TOK), F32),
            pltpu.VMEM((PLANE, 384, TOK), F32),
            pltpu.VMEM((TOK, 128), F32),
            pltpu.VMEM((384, 128), F32),
            pltpu.VMEM((TOK, 128), F32),
            pltpu.VMEM((384, 128), F32),
        ],
    )(sc, queries, qa, qb, qc, *kvs)
    ra = lax.ppermute(pay_a, "z", back(MID_GO))
    rb = lax.ppermute(pay_b, "z", back(B_GO))
    rc = lax.ppermute(pay_c, "z", back(C_GO))
    o_all, mixed, st_all = call(
        combine_kernel, [((TOK, 192), F32), ((TOK, 192), BF16), ((TOK, 128), F32)]
    )(sc, o_near, st_near, ra, rb, rc)

    attended = jnp.concatenate(gather_over_tensor(mixed), 1).astype(F32)
    mix_normed, mix_unit, mix_scale = norm_rows(attended, gain_full, shift_full)
    mix_low = mix_normed.astype(BF16)
    branch = jnp.einsum("te,de->td", mix_low, out_full, preferred_element_type=F32)
    hidden = source + branch
    mid_normed, mid_unit, mid_scale = norm_rows(hidden, mid_gain, mid_shift)
    mid_low = mid_normed.astype(BF16)
    pre_act = jnp.dot(mid_low, up_weight, preferred_element_type=F32)
    active = smooth(pre_act)

    upstream = jnp.where(row_valid, cotangent.astype(F32), 0.0)
    feed_grad = upstream.astype(BF16)
    inner_grad = jnp.einsum("td,fd->tf", feed_grad, down_weight, preferred_element_type=F32)
    inner_scaled = inner_grad * inner_gain
    sums = sum_small_over_tensor(
        jnp.stack(
            [
                jnp.sum(active, 1),
                jnp.sum(active * active, 1),
                jnp.sum(inner_scaled, 1),
                jnp.sum(inner_scaled * active, 1),
            ]
        )
    )
    width = 3072
    inner_mean = (sums[0] / width)[:, None]
    inner_scale = lax.rsqrt((sums[1] / width)[:, None] - inner_mean * inner_mean + EPSILON)
    inner_unit = (active - inner_mean) * inner_scale
    inner_low = (inner_unit * inner_gain + inner_shift).astype(BF16)
    first_back = sums[2][:, None]
    second_back = inner_scale * (sums[3][:, None] - inner_mean * first_back)
    active_grad = inner_scale * (inner_scaled - first_back / width - inner_unit * second_back / width)
    pre_grad = jax.vjp(smooth, pre_act)[1](active_grad)[0].astype(BF16)
    mid_part = jnp.einsum("tf,df->td", pre_grad, up_weight, preferred_element_type=F32).astype(BF16)
    mid_grad = sum_over_tensor(mid_part).astype(F32)

    feed_part = jnp.dot(inner_low, down_weight, preferred_element_type=F32).astype(BF16)
    feed_out = sum_over_tensor(feed_part).astype(F32)
    result = jnp.where(row_valid, hidden + feed_out, 0.0).astype(BF16)
    inner_gain_grad = jnp.sum(inner_grad * inner_unit, 0)
    inner_shift_grad = jnp.sum(inner_grad, 0)
    down_grad = jnp.einsum("tf,td->fd", inner_low, feed_grad, preferred_element_type=F32)
    up_grad = jnp.einsum("td,tf->df", mid_low, pre_grad, preferred_element_type=F32)

    mid_gain_grad = jnp.sum(mid_grad * mid_unit, 0)
    mid_shift_grad = jnp.sum(mid_grad, 0)
    hidden_grad = upstream + norm_rows_back(mid_grad, mid_unit, mid_scale, mid_gain)
    branch_grad = hidden_grad.astype(BF16)
    mix_grad = jnp.einsum("td,de->te", branch_grad, out_full, preferred_element_type=F32)
    attended_grad = norm_rows_back(mix_grad, mix_unit, mix_scale, gain_full)
    mine = tensor * 192

    def own_columns(v):
        return lax.dynamic_slice_in_dim(v, mine, 192, 1)

    attended_grad = own_columns(attended_grad).astype(BF16)
    mix_grad_own = own_columns(mix_grad)
    mix_gain_grad = jnp.sum(mix_grad_own * own_columns(mix_unit), 0)
    mix_shift_grad = jnp.sum(mix_grad_own, 0)
    out_grad = jnp.einsum("te,td->ed", own_columns(mix_low), branch_grad, preferred_element_type=F32)

    st_near, pay_a, pay_b, pay_c = call(
        prepare_kernel, [((TOK, 128), F32)] + [((SLOTS, 256), BF16)] * 3
    )(sc, attended_grad, o_all, st_all)
    ga = lax.ppermute(pay_a, "z", MID_GO)
    gb = lax.ppermute(pay_b, "z", B_GO)
    gc = lax.ppermute(pay_c, "z", C_GO)

    ff_grads = jnp.concatenate([down_grad.astype(BF16), up_grad.astype(BF16), out_grad.astype(BF16), jnp.zeros((320, 768), BF16)], 0)
    ff_grads = sum_over_seq(ff_grads)

    out = call(
        backward_kernel,
        [((TOK, 192), F32)] + [((SLOTS, 256), BF16)] * 3 + [((384, TOK), BF16)] * PLANE,
        [
            pltpu.VMEM((640, 128), BF16),
            pltpu.VMEM((640, 128), BF16),
            pltpu.VMEM((128, 640), BF16),
            pltpu.VMEM((640, HDIM), F32),
            pltpu.VMEM((128, TOK), F32),
        ],
    )(sc, queries, qa, qb, qc, attended_grad, st_near, ga, gb, gc, loc, *kvs)
    dq_near, pay_a, pay_b, pay_c = out[:4]
    ra = lax.ppermute(pay_a, "z", back(MID_GO))
    rb = lax.ppermute(pay_b, "z", back(B_GO))
    rc = lax.ppermute(pay_c, "z", back(C_GO))
    dkv = out[4].astype(F32)
    for k in range(1, PLANE):
        dkv += lax.ppermute(
            out[4 + k], ("yh", "x"), [(i, (i - k) % PLANE) for i in range(PLANE)]
        ).astype(F32)
    dkv = dkv.astype(BF16).reshape(2, 192, TOK)
    (dq,) = call(collect_kernel, [((TOK, 192), BF16)])(sc, dq_near, ra, rb, rc)

    head_grad = jnp.stack(
        [
            jnp.einsum("td,te->de", normed_low, dq, preferred_element_type=F32),
            jnp.einsum("td,et->de", normed_low, dkv[0], preferred_element_type=F32),
            jnp.einsum("td,et->de", normed_low, dkv[1], preferred_element_type=F32),
        ]
    ).astype(BF16)
    normed_part = (
        jnp.einsum("te,de->td", dq, head_weights[0], preferred_element_type=F32)
        + jnp.einsum("et,de->td", dkv[0], head_weights[1], preferred_element_type=F32)
        + jnp.einsum("et,de->td", dkv[1], head_weights[2], preferred_element_type=F32)
    )
    normed_grad = sum_over_tensor(normed_part.astype(BF16)).astype(F32)
    inputs_grad = (hidden_grad + norm_rows_back(normed_grad, in_unit, in_scale, in_gain)).astype(BF16)
    in_sums = sum_small_over_tensor(jnp.stack([jnp.sum(normed_part * in_unit, 0), jnp.sum(normed_part, 0)]))

    pad = jnp.zeros((576,), F32)
    small = jnp.concatenate(
        [
            in_sums.reshape(-1),
            mid_gain_grad,
            mid_shift_grad,
            inner_gain_grad,
            inner_shift_grad,
            mix_gain_grad,
            mix_shift_grad,
            pad,
            pad,
        ]
    ).astype(BF16)
    small = jnp.concatenate([small, jnp.zeros((320 * 256 - small.shape[0],), BF16)])
    last = jnp.concatenate([head_grad.reshape(1728, 256), small.reshape(320, 256)], 0)
    last = sum_over_seq(last).astype(F32)
    head_grad = last[:1728].reshape(3, 768, 192)
    small = last[1728:].reshape(-1)
    ff_grads = ff_grads.astype(F32)
    vec = [small[i * 768 : (i + 1) * 768] for i in range(6)]
    return (
        result,
        inputs_grad,
        head_grad,
        ff_grads[1536:1728],
        ff_grads[768:1536],
        ff_grads[:768],
        vec[0],
        vec[1],
        small[4608:4800],
        small[4800:4992],
        vec[2],
        vec[3],
        vec[4],
        vec[5],
    )


def solution(mesh):
    fine = Mesh(np.asarray(mesh.devices).reshape(4, 2, 4, 2, 2), SEQ + TENSOR)
    in_specs = (
        P(SEQ, None),
        P(None, None, TENSOR),
        P(TENSOR, None),
        P(None, TENSOR),
        P(TENSOR, None),
        P(),
        P(),
        P(TENSOR),
        P(TENSOR),
        P(),
        P(),
        P(TENSOR),
        P(TENSOR),
        P(),
        P(SEQ, None),
    )
    out_specs = (
        P(SEQ, None),
        P(SEQ, None),
        P(None, None, TENSOR),
        P(TENSOR, None),
        P(None, TENSOR),
        P(TENSOR, None),
        P(),
        P(),
        P(TENSOR),
        P(TENSOR),
        P(),
        P(),
        P(TENSOR),
        P(TENSOR),
    )
    return jax.shard_map(per_device, mesh=fine, in_specs=in_specs, out_specs=out_specs, check_vma=False)
```

time: 1110 us -> 485 us (0.44)
  waiting for transfers between devices: 591 us -> 174 us
  blocking collectives: 209 us -> 0 us
  starting transfers between devices: 0.59 us -> 166 us
  matrix products: 169 us -> 13.9 us
  other arithmetic: 104 us -> 41.3 us
  Pallas kernels: 0 us -> 37.4 us
  local copies, waits for them, and re-layouts: 4.68 us -> 26.1 us
    psum x4 -> x0, waiting for transfers between devices: 277 us -> none  [the longest x1 175 us: per_device(): lax.psum(head_grad.astype(jnp.bfloat16), 'seq').astype(jnp.float32)]
    reduce_scatter x1 -> x0, waiting for transfers between devices: 220 us -> none  [per_device(): lax.psum_scatter(pair_terms.astype(jnp.bfloat16), 'seq', scatter_dimensio...]
    psum x5 -> x0, blocking collectives: 209 us -> none  [the longest x1 184 us: per_device(): lax.psum(in_gain_grad.astype(jnp.bfloat16), 'seq').astype(jnp.float32)]
    ppermute x0 -> x122, waiting for transfers between devices: none -> 174 us  [the longest x40 83.7 us: sum_over_seq(): parts[j] = keep + lax.ppermute(send, axis, perm)]
    ppermute x0 -> x122, starting transfers between devices: none -> 166 us  [the longest x40 55.4 us: sum_over_seq(): other = lax.ppermute(parts[j], axis, perm)]
    dot_general x29 -> x17, matrix products: 168 us -> 11.9 us  [the longest x1 1.95 us: per_device(): jnp.dot(inner_low, down_weight, preferred_element_type=F32).astype(BF16)]
    all_gather x1, waiting for transfers between devices: 93.8 us -> 0.02 us  [per_device(): packed = lax.all_gather(packed, TENSOR, axis=0)]
    reduce_sum x9 -> x6, other arithmetic: 47.9 us -> 8.49 us  [the longest x2 2.62 us: norm_rows(): mean = jnp.sum(v, 1, keepdims=True) / v.shape[1]]
  transfers between devices with their start and end apart: 6 -> 123, of which waited for: 6 -> 66; matrix products, arithmetic and copies ran while one was open for 3% -> 12% of each run, Pallas kernels for 0% -> 8%
where the time goes in v1:
time: 485 us; the launch traced here: 476 us
  waiting for transfers between devices  174 us (36%)
  starting transfers between devices  166 us (34%)
  other arithmetic  41.3 us (9%)
  Pallas kernels  37.4 us (8%)
  local copies, waits for them, and re-layouts  26.1 us (5%)
  between operations  17.3 us (4%)
  matrix products  13.9 us (3%)
    ppermute x40, waiting for transfers between devices, sum_over_seq(): parts[j] = keep + lax.ppermute(send, axis, perm)  83.7 us
    ppermute x40, starting transfers between devices, sum_over_seq(): other = lax.ppermute(parts[j], axis, perm)  55.4 us
    ppermute x40, starting transfers between devices, sum_over_seq(): parts[j] = keep + lax.ppermute(send, axis, perm)  47 us
    ppermute x40, waiting for transfers between devices, sum_over_seq(): other = lax.ppermute(parts[j], axis, perm)  44.1 us
    pallas_call x5, Pallas kernels, run(): pl.pallas_call(kernel, out_shape=[jax.ShapeDtypeStruct(s, d) for s, d in...  37.4 us
    ppermute x7, starting transfers between devices, per_device(): lax.ppermute(out[4 + k], ('yh', 'x'), [(i, (i - k) % PLANE) for i in rang...  22.9 us
    select_n x40, other arithmetic, sum_over_seq(): jnp.where(side == 0, jnp.concatenate([parts[j], other]), jnp.concatenate(...  16.6 us
    ppermute x7, waiting for transfers between devices, per_device(): lax.ppermute(pairs, ('yh', 'x'), [(i, (i + k) % PLANE) for i in range(PLA...  15.8 us
  transfers between devices with their start and end apart: 123, of which 66 were waited for; matrix products, arithmetic and copies ran while one was open for 12% of the time, Pallas kernels for 8%

profile of v1, /device:TPU:0, one launch (start us, length us, event | category | flops | bytes accessed | tf_op | source)
XLA Modules:
  0.0 476.1 jit_solution(7664789017793101279)
XLA Ops:
  10.6 5.5 %collective-permute-start.9 = (bf16[384,256]{1,0:T(8,128)(2,1)S(1)}, bf16[384,256]{1,0:T(8,128)(2,1)S(1)}, u32[]{:S(2)}, u32[]{:S(2)}) collective-permute-start(bf16[384,256]{1,0:T(8,128)(2,1)S(1)} %bitcast.65), channel_id=1, source_target_pairs={{0,28},{4,0},{8,4},{12,8},{16,12},{20,16},{24,20},{28,24},{1,29},{... | collective-permute-start | bytes 589832 | tf_op jit(solution)/shard_map/ppermute | solution.py:466
  25.5 3.5 collective-permute-done.2.qc
  30.7 4.2 collective-permute-start.4
  36.9 15.8 %collective-permute-done.6.refs_4_ = bf16[384,256]{1,0:T(8,128)(2,1)S(1)} collective-permute-done((bf16[384,256]{1,0:T(8,128)(2,1)S(1)}, bf16[384,256]{1,0:T(8,128)(2,1)S(1)}, u32[]{:S(2)}, u32[]{:S(2)}) %collective-permute-start.6) | collective-permute-done | bytes 196640 | tf_op jit(solution)/shard_map/ppermute | solution.py:466
  52.6 14.1 %shard_map.254 = (f32[256,192]{1,0:T(8,128)S(1)}, f32[256,128]{1,0:T(8,128)S(1)}, bf16[128,256]{1,0:T(8,128)(2,1)S(1)}, bf16[128,256]{1,0:T(8,128)(2,1)S(1)}, bf...) custom-call(s32[5]{0:T(128)S(1)} %stack.97.sc, bf16[192,256]{1,0:T(8,128)(2,1)S(1)} %get-tuple-element.144.q, ...), custom_call_target="tpu_custom_call" | custom-call | tf_op jit(solution)/shard_map/pallas_call | solution.py:312
  73.4 4.9 %shard_map.255 = (f32[256,192]{1,0:T(8,128)S(1)}, bf16[256,192]{1,0:T(8,128)(2,1)}, f32[256,128]{1,0:T(8,128)S(1)}) custom-call(s32[5]{0:T(128)S(1)} %stack.97.sc, f32[256,192]{1,0:T(8,128)S(1)} %get-tuple-element.39.o_near, f32[256,128]{1,0:T(8,128)S(1)} %get-tuple-element.40.st_near, bf16[128,256]{1,0:T(8,128)(2,1)S(1)} %collective-permute-done.10.ra, ...), custom_call_target="tpu_custom_call" | custom-call | tf_op jit(solution)/shard_map/pallas_call | solution.py:312
  80.9 3.3 collective-permute-done.14
  116.3 6.7 %collective-permute-done.92 = bf16[256,768]{1,0:T(8,128)(2,1)S(1)} collective-permute-done((bf16[256,768]{1,0:T(8,128)(2,1)S(1)}, bf16[256,768]{1,0:T(8,128)(2,1)S(1)}, u32[]{:S(2)}, u32[]{:S(2)}) %collective-permute-start.92) | collective-permute-done | bytes 393248 | tf_op jit(solution)/shard_map/ppermute | solution.py:375
  124.9 3.6 collective-permute-start.103
  153.7 3.1 collective-permute-done.26.pay_c
  156.7 15.5 %shard_map.257 = (f32[256,192]{1,0:T(8,128)S(1)}, bf16[128,256]{1,0:T(8,128)(2,1)S(1)}, bf16[128,256]{1,0:T(8,128)(2,1)S(1)}, bf16[128,256]{1,0:T(8,128)(2,1)S(1...) custom-call(s32[5]{0:T(128)S(1)} %stack.97.sc, ...), custom_call_target="tpu_custom_call" | custom-call | tf_op jit(solution)/shard_map/pallas_call | solution.py:312
  177.7 15.0 %collective-permute-start.30 = (bf16[384,256]{1,0:T(8,128)(2,1)S(1)}, bf16[384,256]{1,0:T(8,128)(2,1)S(1)}, u32[]{:S(2)}, u32[]{:S(2)}) collective-permute-start(bf16[384,256]{1,0:T(8,128)(2,1)S(1)} %get-tuple-element.57), channel_id=1, source_target_pairs={{0,28},{4,0},{8,4},{12,8},{16,12},{20,16},{24,20},{28,24},{1,29},{... | collective-permute-start | bytes 589832 | tf_op jit(solution)/shard_map/ppermute | solution.py:585
  193.1 3.2 collective-permute-start.105
  197.8 4.7 collective-permute-done.105
  203.0 3.2 collective-permute-start.106
  208.4 3.2 collective-permute-start.97
  213.7 3.2 collective-permute-start.87
  224.3 3.2 collective-permute-start.33
  234.1 5.8 %collective-permute-done.33 = bf16[384,256]{1,0:T(8,128)(2,1)S(1)} collective-permute-done((bf16[384,256]{1,0:T(8,128)(2,1)S(1)}, bf16[384,256]{1,0:T(8,128)(2,1)S(1)}, u32[]{:S(2)}, u32[]{:S(2)}) %collective-permute-start.33) | collective-permute-done | bytes 196640 | tf_op jit(solution)/shard_map/ppermute | solution.py:585
  257.8 3.3 collective-permute-start.90
  262.1 3.5 collective-permute-done.51
  265.9 5.2 %collective-permute-done.61 = bf16[128,256]{1,0:T(8,128)(2,1)S(1)} collective-permute-done((bf16[128,256]{1,0:T(8,128)(2,1)S(1)}, bf16[128,256]{1,0:T(8,128)(2,1)S(1)}, u32[]{:S(2)}, u32[]{:S(2)}) %collective-permute-start.61) | collective-permute-done | bytes 65568 | tf_op jit(solution)/shard_map/ppermute | solution.py:375
  271.1 5.4 %collective-permute-done.41 = bf16[128,256]{1,0:T(8,128)(2,1)S(1)} collective-permute-done((bf16[128,256]{1,0:T(8,128)(2,1)S(1)}, bf16[128,256]{1,0:T(8,128)(2,1)S(1)}, u32[]{:S(2)}, u32[]{:S(2)}) %collective-permute-start.41) | collective-permute-done | bytes 65568 | tf_op jit(solution)/shard_map/ppermute | solution.py:375
  277.1 4.6 collective-permute-done.52
  281.8 3.9 collective-permute-done.62
  286.5 3.1 collective-permute-done.42
  293.5 4.9 %collective-permute-done.63 = bf16[32,256]{1,0:T(8,128)(2,1)S(1)} collective-permute-done((bf16[32,256]{1,0:T(8,128)(2,1)S(1)}, bf16[32,256]{1,0:T(8,128)(2,1)S(1)}, u32[]{:S(2)}, u32[]{:S(2)}) %collective-permute-start.63) | collective-permute-done | bytes 16416 | tf_op jit(solution)/shard_map/ppermute | solution.py:375
  298.9 4.5 collective-permute-done.43
  303.4 4.0 collective-permute-start.54
  309.0 3.5 collective-permute-start.64
  314.1 3.5 collective-permute-start.44
  319.3 3.5 collective-permute-start.55
  324.6 3.4 collective-permute-start.65
  329.7 3.4 collective-permute-start.45
  354.0 3.2 collective-permute-start.101
  357.4 4.2 collective-permute-done.58
  362.8 4.2 collective-permute-done.68
  367.7 5.1 %collective-permute-done.114 = bf16[64,768]{1,0:T(8,128)(2,1)S(1)} collective-permute-done((bf16[64,768]{1,0:T(8,128)(2,1)S(1)}, bf16[64,768]{1,0:T(8,128)(2,1)S(1)}, u32[]{:S(2)}, u32[]{:S(2)}) %collective-permute-start.114) | collective-permute-done | bytes 98336 | tf_op jit(solution)/shard_map/ppermute | solution.py:375
  372.9 5.4 %collective-permute-done.48 = bf16[128,256]{1,0:T(8,128)(2,1)S(1)} collective-permute-done((bf16[128,256]{1,0:T(8,128)(2,1)S(1)}, bf16[128,256]{1,0:T(8,128)(2,1)S(1)}, u32[]{:S(2)}, u32[]{:S(2)}) %collective-permute-start.48) | collective-permute-done | bytes 65568 | tf_op jit(solution)/shard_map/ppermute | solution.py:379
  378.6 3.9 collective-permute-done.115
  386.2 3.8 collective-permute-start.116
  395.5 3.5 concatenate.330
  405.5 3.5 collective-permute-start.117
  410.1 3.3 collective-permute-done.73
  415.0 3.7 collective-permute-done.74
  418.9 3.3 collective-permute-start.119
  424.0 3.9 collective-permute-done.76
  438.4 3.6 collective-permute-done.79
  (525 shorter events, 223.1 us)
Async XLA Ops:
  7.2 82.3 %all-gather.4.cloned.1.call-start = ((), (), s32[]{:S(2)}) async-start(), calls=%async_computation | async-start | bytes 1720320 | tf_op jit(solution)/shard_map/all_gather | solution.py:453
  10.6 20.1 %collective-permute-start.9 = (bf16[384,256]{1,0:T(8,128)(2,1)S(1)}, bf16[384,256]{1,0:T(8,128)(2,1)S(1)}, u32[]{:S(2)}, u32[]{:S(2)}) collective-permute-start(bf16[384,256]{1,0:T(8,128)(2,1)S(1)} %bitcast.65), channel_id=1, source_target_pairs={{0,28},{4,0},{8,4},{12,8},{16,12},{20,16},{24,20},{28,24},{1,29},{... | collective-permute-start | bytes 589832 | tf_op jit(solution)/shard_map/ppermute | solution.py:466
  16.1 18.8 %collective-permute-start.8 = (bf16[384,256]{1,0:T(8,128)(2,1)S(1)}, bf16[384,256]{1,0:T(8,128)(2,1)S(1)}, u32[]{:S(2)}, u32[]{:S(2)}) collective-permute-start(bf16[384,256]{1,0:T(8,128)(2,1)S(1)} %bitcast.66), channel_id=1, source_target_pairs={{0,24},{4,28},{8,0},{12,4},{16,8},{20,12},{24,16},{28,20},{1,25},{... | collective-permute-start | bytes 589832 | tf_op jit(solution)/shard_map/ppermute | solution.py:466
  20.5 8.5 %collective-permute-start.2 = (bf16[192,128]{1,0:T(8,128)(2,1)S(1)}, bf16[192,128]{1,0:T(8,128)(2,1)S(1)}, u32[]{:S(2)}, u32[]{:S(2)}) collective-permute-start(bf16[192,128]{1,0:T(8,128)(2,1)S(1)} %bitcast.103), channel_id=1, source_target_pairs={{96,0},{64,32},{97,1},{65,33},{98,2},{66,34},{99,3},{67,35},{100,4... | collective-permute-start | bytes 147464 | tf_op jit(solution)/shard_map/ppermute | solution.py:475
  21.8 8.7 %collective-permute-start.1 = (bf16[192,128]{1,0:T(8,128)(2,1)S(1)}, bf16[192,128]{1,0:T(8,128)(2,1)S(1)}, u32[]{:S(2)}, u32[]{:S(2)}) collective-permute-start(bf16[192,128]{1,0:T(8,128)(2,1)S(1)} %bitcast.104), channel_id=1, source_target_pairs={{64,0},{96,32},{65,1},{97,33},{66,2},{98,34},{67,3},{99,35},{68,4}... | collective-permute-start | bytes 147464 | tf_op jit(solution)/shard_map/ppermute | solution.py:474
  24.8 12.0 %collective-permute-start.7 = (bf16[384,256]{1,0:T(8,128)(2,1)S(1)}, bf16[384,256]{1,0:T(8,128)(2,1)S(1)}, u32[]{:S(2)}, u32[]{:S(2)}) collective-permute-start(bf16[384,256]{1,0:T(8,128)(2,1)S(1)} %bitcast.67), channel_id=1, source_target_pairs={{0,20},{4,24},{8,28},{12,0},{16,4},{20,8},{24,12},{28,16},{1,21},{... | collective-permute-start | bytes 589832 | tf_op jit(solution)/shard_map/ppermute | solution.py:466
  29.0 23.6 %collective-permute-start.6 = (bf16[384,256]{1,0:T(8,128)(2,1)S(1)}, bf16[384,256]{1,0:T(8,128)(2,1)S(1)}, u32[]{:S(2)}, u32[]{:S(2)}) collective-permute-start(bf16[384,256]{1,0:T(8,128)(2,1)S(1)} %bitcast.68), channel_id=1, source_target_pairs={{0,16},{4,20},{8,24},{12,28},{16,0},{20,4},{24,8},{28,12},{1,17},{... | collective-permute-start | bytes 589832 | tf_op jit(solution)/shard_map/ppermute | solution.py:466
  30.4 22.2 %collective-permute-start.5 = (bf16[384,256]{1,0:T(8,128)(2,1)S(1)}, bf16[384,256]{1,0:T(8,128)(2,1)S(1)}, u32[]{:S(2)}, u32[]{:S(2)}) collective-permute-start(bf16[384,256]{1,0:T(8,128)(2,1)S(1)} %bitcast.69), channel_id=1, source_target_pairs={{0,12},{4,16},{8,20},{12,24},{16,28},{20,0},{24,4},{28,8},{1,13},{... | collective-permute-start | bytes 589832 | tf_op jit(solution)/shard_map/ppermute | solution.py:466
  30.7 21.9 %collective-permute-start.4 = (bf16[384,256]{1,0:T(8,128)(2,1)S(1)}, bf16[384,256]{1,0:T(8,128)(2,1)S(1)}, u32[]{:S(2)}, u32[]{:S(2)}) collective-permute-start(bf16[384,256]{1,0:T(8,128)(2,1)S(1)} %bitcast.70), channel_id=1, source_target_pairs={{0,8},{4,12},{8,16},{12,20},{16,24},{20,28},{24,0},{28,4},{1,9},{5... | collective-permute-start | bytes 589832 | tf_op jit(solution)/shard_map/ppermute | solution.py:466
  34.9 17.7 %collective-permute-start.3 = (bf16[384,256]{1,0:T(8,128)(2,1)S(1)}, bf16[384,256]{1,0:T(8,128)(2,1)S(1)}, u32[]{:S(2)}, u32[]{:S(2)}) collective-permute-start(bf16[384,256]{1,0:T(8,128)(2,1)S(1)} %bitcast.71), channel_id=1, source_target_pairs={{0,4},{4,8},{8,12},{12,16},{16,20},{20,24},{24,28},{28,0},{1,5},{5... | collective-permute-start | bytes 589832 | tf_op jit(solution)/shard_map/ppermute | solution.py:466
  110.7 12.3 %collective-permute-start.92 = (bf16[256,768]{1,0:T(8,128)(2,1)S(1)}, bf16[256,768]{1,0:T(8,128)(2,1)S(1)}, u32[]{:S(2)}, u32[]{:S(2)}) collective-permute-start(bf16[256,768]{1,0:T(8,128)(2,1)S(1)} %fusion.39), channel_id=1, source_target_pairs={{0,12},{12,0},{4,8},{8,4},{1,13},{13,1},{5,9},{9,5},{2,14},{14,2},... | collective-permute-start | bytes 1179656 | tf_op jit(solution)/shard_map/ppermute | solution.py:375
  110.8 14.0 %collective-permute-start.102 = (bf16[256,768]{1,0:T(8,128)(2,1)S(1)}, bf16[256,768]{1,0:T(8,128)(2,1)S(1)}, u32[]{:S(2)}, u32[]{:S(2)}) collective-permute-start(bf16[256,768]{1,0:T(8,128)(2,1)S(1)} %constant_dynamic-slice_fusion.8), channel_id=1, source_target_pairs={{0,32},{32,0},{64,96},{96,64},{1,33},{33,1},{65,97},{97,65},{2,34}... | collective-permute-start | bytes 1179656 | tf_op jit(solution)/shard_map/ppermute | solution.py:375
  111.4 17.2 %collective-permute-start.82 = (bf16[256,768]{1,0:T(8,128)(2,1)S(1)}, bf16[256,768]{1,0:T(8,128)(2,1)S(1)}, u32[]{:S(2)}, u32[]{:S(2)}) collective-permute-start(bf16[256,768]{1,0:T(8,128)(2,1)S(1)} %constant_dynamic-slice_fusion.17), channel_id=1, source_target_pairs={{0,4},{4,0},{8,12},{12,8},{1,5},{5,1},{9,13},{13,9},{2,6},{6,2},{1... | collective-permute-start | bytes 1179656 | tf_op jit(solution)/shard_map/ppermute | solution.py:375
  114.0 15.7 %collective-permute-start.22 = (bf16[128,768]{1,0:T(8,128)(2,1)S(1)}, bf16[128,768]{1,0:T(8,128)(2,1)S(1)}, u32[]{:S(2)}, u32[]{:S(2)}) collective-permute-start(bf16[128,768]{1,0:T(8,128)(2,1)S(1)} %dynamic-slice_add_fusion.7), channel_id=1, source_target_pairs={{0,2},{2,0},{1,3},{3,1},{4,6},{6,4},{5,7},{7,5},{8,10},{10,8},{9,1... | collective-permute-start | bytes 589832 | tf_op jit(solution)/shard_map/ppermute | solution.py:392
  114.8 15.0 %collective-permute-start.19 = (bf16[128,768]{1,0:T(8,128)(2,1)S(1)}, bf16[128,768]{1,0:T(8,128)(2,1)S(1)}, u32[]{:S(2)}, u32[]{:S(2)}) collective-permute-start(bf16[128,768]{1,0:T(8,128)(2,1)S(1)} %dynamic-slice_add_fusion.8), channel_id=1, source_target_pairs={{0,2},{2,0},{1,3},{3,1},{4,6},{6,4},{5,7},{7,5},{8,10},{10,8},{9,1... | collective-permute-start | bytes 589832 | tf_op jit(solution)/shard_map/ppermute | solution.py:392
  130.6 45.7 %collective-permute-start.94 = (bf16[64,768]{1,0:T(8,128)(2,1)S(1)}, bf16[64,768]{1,0:T(8,128)(2,1)S(1)}, u32[]{:S(2)}, u32[]{:S(2)}) collective-permute-start(bf16[64,768]{1,0:T(8,128)(2,1)S(1)} %constant_dynamic-slice_fusion.11), channel_id=1, source_target_pairs={{0,96},{96,0},{32,64},{64,32},{1,97},{97,1},{33,65},{65,33},{2,98}... | collective-permute-start | bytes 294920 | tf_op jit(solution)/shard_map/ppermute | solution.py:375
  133.4 44.2 %collective-permute-start.104 = (bf16[64,768]{1,0:T(8,128)(2,1)S(1)}, bf16[64,768]{1,0:T(8,128)(2,1)S(1)}, u32[]{:S(2)}, u32[]{:S(2)}) collective-permute-start(bf16[64,768]{1,0:T(8,128)(2,1)S(1)} %constant_dynamic-slice_fusion.6), channel_id=1, source_target_pairs={{0,4},{4,0},{8,12},{12,8},{1,5},{5,1},{9,13},{13,9},{2,6},{6,2},{1... | collective-permute-start | bytes 294920 | tf_op jit(solution)/shard_map/ppermute | solution.py:375
  147.3 9.4 %collective-permute-start.26 = (bf16[128,256]{1,0:T(8,128)(2,1)S(1)}, bf16[128,256]{1,0:T(8,128)(2,1)S(1)}, u32[]{:S(2)}, u32[]{:S(2)}) collective-permute-start(bf16[128,256]{1,0:T(8,128)(2,1)S(1)} %get-tuple-element.50), channel_id=1, source_target_pairs={{96,0},{64,32},{97,1},{65,33},{98,2},{66,34},{99,3},{67,35},{100,4... | collective-permute-start | bytes 196616 | tf_op jit(solution)/shard_map/ppermute | solution.py:563
  150.9 41.8 %collective-permute-start.84 = (bf16[64,768]{1,0:T(8,128)(2,1)S(1)}, bf16[64,768]{1,0:T(8,128)(2,1)S(1)}, u32[]{:S(2)}, u32[]{:S(2)}) collective-permute-start(bf16[64,768]{1,0:T(8,128)(2,1)S(1)} %constant_dynamic-slice_fusion.15), channel_id=1, source_target_pairs={{0,32},{32,0},{64,96},{96,64},{1,33},{33,1},{65,97},{97,65},{2,34}... | collective-permute-start | bytes 294920 | tf_op jit(solution)/shard_map/ppermute | solution.py:375
  172.2 20.7 %collective-permute-start.27 = (bf16[128,256]{1,0:T(8,128)(2,1)S(1)}, bf16[128,256]{1,0:T(8,128)(2,1)S(1)}, u32[]{:S(2)}, u32[]{:S(2)}) collective-permute-start(bf16[128,256]{1,0:T(8,128)(2,1)S(1)} %get-tuple-element.53), channel_id=1, source_target_pairs={{0,32},{64,96},{1,33},{65,97},{2,34},{66,98},{3,35},{67,99},{4,36}... | collective-permute-start | bytes 196616 | tf_op jit(solution)/shard_map/ppermute | solution.py:580
  174.2 18.8 %collective-permute-start.28 = (bf16[128,256]{1,0:T(8,128)(2,1)S(1)}, bf16[128,256]{1,0:T(8,128)(2,1)S(1)}, u32[]{:S(2)}, u32[]{:S(2)}) collective-permute-start(bf16[128,256]{1,0:T(8,128)(2,1)S(1)} %get-tuple-element.54), channel_id=1, source_target_pairs={{0,64},{32,96},{1,65},{33,97},{2,66},{34,98},{3,67},{35,99},{4,68}... | collective-permute-start | bytes 196616 | tf_op jit(solution)/shard_map/ppermute | solution.py:581
  176.3 16.8 %collective-permute-start.29 = (bf16[128,256]{1,0:T(8,128)(2,1)S(1)}, bf16[128,256]{1,0:T(8,128)(2,1)S(1)}, u32[]{:S(2)}, u32[]{:S(2)}) collective-permute-start(bf16[128,256]{1,0:T(8,128)(2,1)S(1)} %get-tuple-element.55), channel_id=1, source_target_pairs={{0,96},{32,64},{1,97},{33,65},{2,98},{34,66},{3,99},{35,67},{4,100... | collective-permute-start | bytes 196616 | tf_op jit(solution)/shard_map/ppermute | solution.py:582
  177.7 51.9 %collective-permute-start.30 = (bf16[384,256]{1,0:T(8,128)(2,1)S(1)}, bf16[384,256]{1,0:T(8,128)(2,1)S(1)}, u32[]{:S(2)}, u32[]{:S(2)}) collective-permute-start(bf16[384,256]{1,0:T(8,128)(2,1)S(1)} %get-tuple-element.57), channel_id=1, source_target_pairs={{0,28},{4,0},{8,4},{12,8},{16,12},{20,16},{24,20},{28,24},{1,29},{... | collective-permute-start | bytes 589832 | tf_op jit(solution)/shard_map/ppermute | solution.py:585
  192.7 39.0 %collective-permute-start.31 = (bf16[384,256]{1,0:T(8,128)(2,1)S(1)}, bf16[384,256]{1,0:T(8,128)(2,1)S(1)}, u32[]{:S(2)}, u32[]{:S(2)}) collective-permute-start(bf16[384,256]{1,0:T(8,128)(2,1)S(1)} %get-tuple-element.58), channel_id=1, source_target_pairs={{0,24},{4,28},{8,0},{12,4},{16,8},{20,12},{24,16},{28,20},{1,25},{... | collective-permute-start | bytes 589832 | tf_op jit(solution)/shard_map/ppermute | solution.py:585
  192.9 40.3 %collective-permute-start.32 = (bf16[384,256]{1,0:T(8,128)(2,1)S(1)}, bf16[384,256]{1,0:T(8,128)(2,1)S(1)}, u32[]{:S(2)}, u32[]{:S(2)}) collective-permute-start(bf16[384,256]{1,0:T(8,128)(2,1)S(1)} %get-tuple-element.59), channel_id=1, source_target_pairs={{0,20},{4,24},{8,28},{12,0},{16,4},{20,8},{24,12},{28,16},{1,21},{... | collective-permute-start | bytes 589832 | tf_op jit(solution)/shard_map/ppermute | solution.py:585
  193.1 9.4 %collective-permute-start.105 = (bf16[32,768]{1,0:T(8,128)(2,1)S(1)}, bf16[32,768]{1,0:T(8,128)(2,1)S(1)}, u32[]{:S(2)}, u32[]{:S(2)}) collective-permute-start(bf16[32,768]{1,0:T(8,128)(2,1)S(1)} %constant_dynamic-slice_fusion.5), channel_id=1, source_target_pairs={{0,12},{12,0},{4,8},{8,4},{1,13},{13,1},{5,9},{9,5},{2,14},{14,2},... | collective-permute-start | bytes 147464 | tf_op jit(solution)/shard_map/ppermute | solution.py:375
  224.3 15.6 %collective-permute-start.33 = (bf16[384,256]{1,0:T(8,128)(2,1)S(1)}, bf16[384,256]{1,0:T(8,128)(2,1)S(1)}, u32[]{:S(2)}, u32[]{:S(2)}) collective-permute-start(bf16[384,256]{1,0:T(8,128)(2,1)S(1)} %get-tuple-element.60), channel_id=1, source_target_pairs={{0,16},{4,20},{8,24},{12,28},{16,0},{20,4},{24,8},{28,12},{1,17},{... | collective-permute-start | bytes 589832 | tf_op jit(solution)/shard_map/ppermute | solution.py:585
  228.5 11.6 %collective-permute-start.34 = (bf16[384,256]{1,0:T(8,128)(2,1)S(1)}, bf16[384,256]{1,0:T(8,128)(2,1)S(1)}, u32[]{:S(2)}, u32[]{:S(2)}) collective-permute-start(bf16[384,256]{1,0:T(8,128)(2,1)S(1)} %get-tuple-element.61), channel_id=1, source_target_pairs={{0,12},{4,16},{8,20},{12,24},{16,28},{20,0},{24,4},{28,8},{1,13},{... | collective-permute-start | bytes 589832 | tf_op jit(solution)/shard_map/ppermute | solution.py:585
  229.6 10.6 %collective-permute-start.35 = (bf16[384,256]{1,0:T(8,128)(2,1)S(1)}, bf16[384,256]{1,0:T(8,128)(2,1)S(1)}, u32[]{:S(2)}, u32[]{:S(2)}) collective-permute-start(bf16[384,256]{1,0:T(8,128)(2,1)S(1)} %get-tuple-element.62), channel_id=1, source_target_pairs={{0,8},{4,12},{8,16},{12,20},{16,24},{20,28},{24,0},{28,4},{1,9},{5... | collective-permute-start | bytes 589832 | tf_op jit(solution)/shard_map/ppermute | solution.py:585
  231.7 10.5 %collective-permute-start.36 = (bf16[384,256]{1,0:T(8,128)(2,1)S(1)}, bf16[384,256]{1,0:T(8,128)(2,1)S(1)}, u32[]{:S(2)}, u32[]{:S(2)}) collective-permute-start(bf16[384,256]{1,0:T(8,128)(2,1)S(1)} %get-tuple-element.63), channel_id=1, source_target_pairs={{0,4},{4,8},{8,12},{12,16},{16,20},{20,24},{24,28},{28,0},{1,5},{5... | collective-permute-start | bytes 589832 | tf_op jit(solution)/shard_map/ppermute | solution.py:585
  233.2 20.1 %collective-permute-start.112 = (bf16[256,768]{1,0:T(8,128)(2,1)}, bf16[256,768]{1,0:T(8,128)(2,1)}, u32[]{:S(2)}, u32[]{:S(2)}) collective-permute-start(bf16[256,768]{1,0:T(8,128)(2,1)} %pad_dynamic-slice_fusion), channel_id=1, source_target_pairs={{0,96},{96,0},{32,64},{64,32},{1,97},{97,1},{33,65},{65,33},{2,98}... | collective-permute-start | bytes 1179656 | tf_op jit(solution)/shard_map/ppermute | solution.py:375
  240.1 12.1 %collective-permute-start.109 = (bf16[64,768]{1,0:T(8,128)(2,1)S(1)}, bf16[64,768]{1,0:T(8,128)(2,1)}, u32[]{:S(2)}, u32[]{:S(2)}) collective-permute-start(bf16[64,768]{1,0:T(8,128)(2,1)S(1)} %maximum_select_fusion.25), channel_id=1, source_target_pairs={{0,4},{4,0},{8,12},{12,8},{1,5},{5,1},{9,13},{13,9},{2,6},{6,2},{1... | collective-permute-start | bytes 294920 | tf_op jit(solution)/shard_map/ppermute | solution.py:379
  240.1 9.9 %collective-permute-start.89 = (bf16[64,768]{1,0:T(8,128)(2,1)S(1)}, bf16[64,768]{1,0:T(8,128)(2,1)}, u32[]{:S(2)}, u32[]{:S(2)}) collective-permute-start(bf16[64,768]{1,0:T(8,128)(2,1)S(1)} %maximum_select_fusion.23), channel_id=1, source_target_pairs={{0,32},{32,0},{64,96},{96,64},{1,33},{33,1},{65,97},{97,65},{2,34}... | collective-permute-start | bytes 294920 | tf_op jit(solution)/shard_map/ppermute | solution.py:379
  248.1 9.7 %collective-permute-start.60 = (bf16[256,256]{1,0:T(8,128)(2,1)S(1)}, bf16[256,256]{1,0:T(8,128)(2,1)S(1)}, u32[]{:S(2)}, u32[]{:S(2)}) collective-permute-start(bf16[256,256]{1,0:T(8,128)(2,1)S(1)} %constant_dynamic-slice_fusion.30), channel_id=1, source_target_pairs={{0,32},{32,0},{64,96},{96,64},{1,33},{33,1},{65,97},{97,65},{2,34}... | collective-permute-start | bytes 393224 | tf_op jit(solution)/shard_map/ppermute | solution.py:375
  250.0 11.2 %collective-permute-start.40 = (bf16[256,256]{1,0:T(8,128)(2,1)S(1)}, bf16[256,256]{1,0:T(8,128)(2,1)S(1)}, u32[]{:S(2)}, u32[]{:S(2)}) collective-permute-start(bf16[256,256]{1,0:T(8,128)(2,1)S(1)} %constant_dynamic-slice_fusion.44), channel_id=1, source_target_pairs={{0,4},{4,0},{8,12},{12,8},{1,5},{5,1},{9,13},{13,9},{2,6},{6,2},{1... | collective-permute-start | bytes 393224 | tf_op jit(solution)/shard_map/ppermute | solution.py:375
  252.2 24.3 %collective-permute-start.37 = (bf16[128,768]{1,0:T(8,128)(2,1)S(1)}, bf16[128,768]{1,0:T(8,128)(2,1)S(1)}, u32[]{:S(2)}, u32[]{:S(2)}) collective-permute-start(bf16[128,768]{1,0:T(8,128)(2,1)S(1)} %constant_dynamic-slice_fusion.45), channel_id=1, source_target_pairs={{0,1},{1,0},{2,3},{3,2},{4,5},{5,4},{6,7},{7,6},{8,9},{9,8},{10,11... | collective-permute-start | bytes 589832 | tf_op jit(solution)/shard_map/ppermute | solution.py:391
  253.3 82.1 %collective-permute-start.100 = (bf16[128,768]{1,0:T(8,128)(2,1)S(1)}, bf16[128,768]{1,0:T(8,128)(2,1)S(1)}, u32[]{:S(2)}, u32[]{:S(2)}) collective-permute-start(bf16[128,768]{1,0:T(8,128)(2,1)S(1)} %maximum_select_fusion.16), channel_id=1, source_target_pairs={{0,4},{4,0},{8,12},{12,8},{1,5},{5,1},{9,13},{13,9},{2,6},{6,2},{1... | collective-permute-start | bytes 589832 | tf_op jit(solution)/shard_map/ppermute | solution.py:379
  255.5 80.1 %collective-permute-start.110 = (bf16[128,768]{1,0:T(8,128)(2,1)S(1)}, bf16[128,768]{1,0:T(8,128)(2,1)S(1)}, u32[]{:S(2)}, u32[]{:S(2)}) collective-permute-start(bf16[128,768]{1,0:T(8,128)(2,1)S(1)} %maximum_select_fusion.17), channel_id=1, source_target_pairs={{0,96},{96,0},{32,64},{64,32},{1,97},{97,1},{33,65},{65,33},{2,98}... | collective-permute-start | bytes 589832 | tf_op jit(solution)/shard_map/ppermute | solution.py:379
  257.8 78.0 %collective-permute-start.90 = (bf16[128,768]{1,0:T(8,128)(2,1)S(1)}, bf16[128,768]{1,0:T(8,128)(2,1)S(1)}, u32[]{:S(2)}, u32[]{:S(2)}) collective-permute-start(bf16[128,768]{1,0:T(8,128)(2,1)S(1)} %maximum_select_fusion.15), channel_id=1, source_target_pairs={{0,12},{12,0},{4,8},{8,4},{1,13},{13,1},{5,9},{9,5},{2,14},{14,2},... | collective-permute-start | bytes 589832 | tf_op jit(solution)/shard_map/ppermute | solution.py:379
  276.5 80.7 %collective-permute-start.113 = (bf16[128,768]{1,0:T(8,128)(2,1)S(1)}, bf16[128,768]{1,0:T(8,128)(2,1)S(1)}, u32[]{:S(2)}, u32[]{:S(2)}) collective-permute-start(bf16[128,768]{1,0:T(8,128)(2,1)S(1)} %constant_dynamic-slice_fusion.3), channel_id=1, source_target_pairs={{0,32},{32,0},{64,96},{96,64},{1,33},{33,1},{65,97},{97,65},{2,34}... | collective-permute-start | bytes 589832 | tf_op jit(solution)/shard_map/ppermute | solution.py:375
  334.9 43.5 %collective-permute-start.38 = (bf16[128,768]{1,0:T(8,128)(2,1)S(1)}, bf16[128,768]{1,0:T(8,128)(2,1)S(1)}, u32[]{:S(2)}, u32[]{:S(2)}) collective-permute-start(bf16[128,768]{1,0:T(8,128)(2,1)S(1)} %dynamic-slice_add_fusion.6), channel_id=1, source_target_pairs={{0,2},{2,0},{1,3},{3,1},{4,6},{6,4},{5,7},{7,5},{8,10},{10,8},{9,1... | collective-permute-start | bytes 589832 | tf_op jit(solution)/shard_map/ppermute | solution.py:392
  339.2 97.8 %collective-permute-start.111 = (bf16[256,768]{1,0:T(8,128)(2,1)S(1)}, bf16[256,768]{1,0:T(8,128)(2,1)}, u32[]{:S(2)}, u32[]{:S(2)}) collective-permute-start(bf16[256,768]{1,0:T(8,128)(2,1)S(1)} %maximum_select_fusion.9), channel_id=1, source_target_pairs={{0,32},{32,0},{64,96},{96,64},{1,33},{33,1},{65,97},{97,65},{2,34}... | collective-permute-start | bytes 1179656 | tf_op jit(solution)/shard_map/ppermute | solution.py:379
  340.9 102.0 %collective-permute-start.91 = (bf16[256,768]{1,0:T(8,128)(2,1)}, bf16[256,768]{1,0:T(8,128)(2,1)}, u32[]{:S(2)}, u32[]{:S(2)}) collective-permute-start(bf16[256,768]{1,0:T(8,128)(2,1)} %maximum_select_fusion.7), channel_id=1, source_target_pairs={{0,4},{4,0},{8,12},{12,8},{1,5},{5,1},{9,13},{13,9},{2,6},{6,2},{1... | collective-permute-start | bytes 1179656 | tf_op jit(solution)/shard_map/ppermute | solution.py:379
  354.0 93.6 %collective-permute-start.101 = (bf16[256,768]{1,0:T(8,128)(2,1)S(1)}, bf16[256,768]{1,0:T(8,128)(2,1)}, u32[]{:S(2)}, u32[]{:S(2)}) collective-permute-start(bf16[256,768]{1,0:T(8,128)(2,1)S(1)} %maximum_select_fusion.8), channel_id=1, source_target_pairs={{0,12},{12,0},{4,8},{8,4},{1,13},{13,1},{5,9},{9,5},{2,14},{14,2},... | collective-permute-start | bytes 1179656 | tf_op jit(solution)/shard_map/ppermute | solution.py:379
  378.4 20.8 %collective-permute-start.59 = (bf16[256,256]{1,0:T(8,128)(2,1)}, bf16[256,256]{1,0:T(8,128)(2,1)}, u32[]{:S(2)}, u32[]{:S(2)}) collective-permute-start(bf16[256,256]{1,0:T(8,128)(2,1)} %maximum_select_fusion.20), channel_id=1, source_target_pairs={{0,12},{12,0},{4,8},{8,4},{1,13},{13,1},{5,9},{9,5},{2,14},{14,2},... | collective-permute-start | bytes 393224 | tf_op jit(solution)/shard_map/ppermute | solution.py:379
  418.9 14.1 %collective-permute-start.119 = (bf16[64,768]{1,0:T(8,128)(2,1)S(1)}, bf16[64,768]{1,0:T(8,128)(2,1)S(1)}, u32[]{:S(2)}, u32[]{:S(2)}) collective-permute-start(bf16[64,768]{1,0:T(8,128)(2,1)S(1)} %maximum_select_fusion.26), channel_id=1, source_target_pairs={{0,12},{12,0},{4,8},{8,4},{1,13},{13,1},{5,9},{9,5},{2,14},{14,2},... | collective-permute-start | bytes 294920 | tf_op jit(solution)/shard_map/ppermute | solution.py:379
  433.1 16.7 %collective-permute-start.120 = (bf16[128,768]{1,0:T(8,128)(2,1)S(1)}, bf16[128,768]{1,0:T(8,128)(2,1)S(1)}, u32[]{:S(2)}, u32[]{:S(2)}) collective-permute-start(bf16[128,768]{1,0:T(8,128)(2,1)S(1)} %maximum_select_fusion.18), channel_id=1, source_target_pairs={{0,32},{32,0},{64,96},{96,64},{1,33},{33,1},{65,97},{97,65},{2,34}... | collective-permute-start | bytes 589832 | tf_op jit(solution)/shard_map/ppermute | solution.py:379
  449.9 14.3 %collective-permute-start.121 = (bf16[256,768]{1,0:T(8,128)(2,1)S(1)}, bf16[256,768]{1,0:T(8,128)(2,1)}, u32[]{:S(2)}, u32[]{:S(2)}) collective-permute-start(bf16[256,768]{1,0:T(8,128)(2,1)S(1)} %maximum_select_fusion.10), channel_id=1, source_target_pairs={{0,96},{96,0},{32,64},{64,32},{1,97},{97,1},{33,65},{65,33},{2,98}... | collective-permute-start | bytes 1179656 | tf_op jit(solution)/shard_map/ppermute | solution.py:379
  (119 other events, 879.6 us)
Sparse Core Ops, SparseCore 0:
  18.6 38.9 all-gather.3
